TPU v7x, 32 devices: a whole 2x2x4 slice. The times are simulated.
32 devices in a mesh: dp: 8 (over z, y), fsdp: 4 (over x, core).
Axes of the slice: x: 2, y: 2, z: 4, core: 2. Of those that a mesh axis runs over, the one named last changes fastest.
Arguments:
- features: bfloat16 [32768, 768], P(('dp', 'fsdp')), may hold values from -6 to 6
- cotangent: bfloat16 [32768, 768], P(('dp', 'fsdp')), may hold values from -6 to 6
- segment_ids: int32 [32768], P(('dp', 'fsdp')), may hold values from -1 to 7, as said below
- attn_weights: float32 [3072, 768], P(('dp', 'fsdp')), may hold values from -0.8660254 to 0.8660254
- ffn_weights: float32 [2, 3072, 768], P(None, ('dp', 'fsdp')), may hold values from -0.21875 to 0.21875
- small_params: float32 [9216], P(('dp', 'fsdp')), may hold values from -0.8 to 1.4
- attn_first: float32 [3072, 768], P(('dp', 'fsdp')), may hold values from -162.9174 to 162.9174
- ffn_first: float32 [2, 3072, 768], P(None, ('dp', 'fsdp')), may hold values from -41.63445 to 41.63445
- small_first: float32 [9216], P(('dp', 'fsdp')), may hold values from -162.9174 to 162.9174
- attn_second: float32 [3072, 768], P(('dp', 'fsdp')), may hold values from 98.304 to 10813.44
- ffn_second: float32 [2, 3072, 768], P(None, ('dp', 'fsdp')), may hold values from 163.84 to 688.128
- small_second: float32 [9216], P(('dp', 'fsdp')), may hold values from 163.84 to 10813.44
- attn_ema: float32 [3072, 768], P(('dp', 'fsdp')), may hold values from -0.21875 to 0.21875
- ffn_ema: float32 [2, 3072, 768], P(None, ('dp', 'fsdp')), may hold values from -0.21875 to 0.21875
- small_ema: float32 [9216], P(('dp', 'fsdp')), may hold values from -3 to 3
Outputs:
- outputs: bfloat16 [32768, 768], P(('dp', 'fsdp'))
- input_grad: float32 [32768, 768], P(('dp', 'fsdp'))
- attn_new: float32 [3072, 768], P(('dp', 'fsdp'))
- ffn_new: float32 [2, 3072, 768], P(None, ('dp', 'fsdp'))
- small_new: float32 [9216], P(('dp', 'fsdp'))
- attn_first_new: float32 [3072, 768], P(('dp', 'fsdp'))
- ffn_first_new: float32 [2, 3072, 768], P(None, ('dp', 'fsdp'))
- small_first_new: float32 [9216], P(('dp', 'fsdp'))
- attn_second_new: float32 [3072, 768], P(('dp', 'fsdp'))
- ffn_second_new: float32 [2, 3072, 768], P(None, ('dp', 'fsdp'))
- small_second_new: float32 [9216], P(('dp', 'fsdp'))
- attn_ema_new: float32 [3072, 768], P(('dp', 'fsdp'))
- ffn_ema_new: float32 [2, 3072, 768], P(None, ('dp', 'fsdp'))
- small_ema_new: float32 [9216], P(('dp', 'fsdp'))
Inputs may be any that keep to these rules, and one draw needn't show every extreme that they name: `segment_ids`: each aligned block of 1024 slots (one device's) holds whole utterances of 128 to 1024 frames, numbered 0, 1, 2, ... in order from the block's start, then padding marked -1 to the block's end; block 0 is one utterance of exactly 1024 frames; the last block holds utterances of exactly 128 frames.
All inputs are finite; a program needn't handle non-finite values.
Results may differ from a plain program's by a relative error of at most 0.015.
The roundings to bfloat16 on the way count: a program that leaves them out, or rounds other values in their place, can miss the bound.
Values may be sent and summed in bfloat16 or wider, within the bound.
A program may use at most 256 MiB of HBM per device.

v0:
```python
from functools import partial

import jax
import jax.numpy as jnp
from jax import lax
from jax.sharding import PartitionSpec as P

D = 768
HEADS = 12
STEP = 10


def layer_norm(residual, gain_vec, bias_vec):
    centre = residual - jnp.mean(residual, axis=-1, keepdims=True)
    spread = jnp.mean(centre * centre, axis=-1, keepdims=True)
    return centre * lax.rsqrt(spread + 1e-05) * gain_vec + bias_vec


def project(left_arg, weight_mat):
    return lax.dot_general(
        left_arg, weight_mat, (((1,), (1,)), ((), ())), preferred_element_type=jnp.float32
    )


def row_outer(left_arg, right_arg):
    return lax.dot_general(
        left_arg, right_arg, (((0,), (0,)), ((), ())), preferred_element_type=jnp.float32
    )


def adam_step(weight, grad_sum, first_mom, second_mom, average, decay, rate):
    first_new = 0.9 * first_mom + 0.1 * grad_sum
    second_new = 0.98 * second_mom + 0.02 * grad_sum * grad_sum
    corrected = first_new / (1.0 - 0.9**STEP)
    denominator = jnp.sqrt(second_new / (1.0 - 0.98**STEP)) + 1e-06
    weight_new = weight - rate * (corrected / denominator + decay * weight)
    average_new = 0.75 * average + 0.25 * weight_new
    return (weight_new, first_new, second_new, average_new)


def local(
    features,
    cotangent,
    segment_ids,
    attn_weights,
    ffn_weights,
    small_params,
    attn_first,
    ffn_first,
    small_first,
    attn_second,
    ffn_second,
    small_second,
    attn_ema,
    ffn_ema,
    small_ema,
):
    rows_here = features.shape[0]
    head_dim = D // HEADS
    score_scale = head_dim ** (-0.5)
    block_rows = min(512, rows_here)
    block_count = rows_here // block_rows
    attn_full, ffn_full, small_full = (
        lax.all_gather(attn_weights.astype(jnp.bfloat16), ("dp", "fsdp"), axis=0, tiled=True),
        lax.all_gather(ffn_weights.astype(jnp.bfloat16), ("dp", "fsdp"), axis=1, tiled=True),
        lax.all_gather(small_params.astype(jnp.bfloat16), ("dp", "fsdp"), axis=0, tiled=True),
    )
    vectors = small_full[: 8 * D].astype(jnp.float32).reshape(8, D)
    hidden_bias = small_full[8 * D :].astype(jnp.float32)
    frames = features.astype(jnp.float32)
    queries = (project(features, attn_full[:D]) + vectors[4]).astype(jnp.bfloat16)
    keys_all = project(features, attn_full[D : 2 * D]).astype(jnp.bfloat16)
    values_all = (project(features, attn_full[2 * D : 3 * D]) + vectors[5]).astype(jnp.bfloat16)
    key_heads = keys_all.reshape(rows_here, HEADS, head_dim)
    value_heads = values_all.reshape(rows_here, HEADS, head_dim)
    query_blocks = queries.reshape(block_count, block_rows, HEADS, head_dim)
    id_blocks = segment_ids.reshape(block_count, block_rows)

    def masked_scores(query_block, id_block):
        scores = (
            jnp.einsum("qhd,khd->hqk", query_block, key_heads, preferred_element_type=jnp.float32)
            * score_scale
        )
        same_utt = (id_block[:, None] == segment_ids[None, :])[None]
        return jnp.where(same_utt, scores, -1000000000.0)

    def attend(block_item):
        query_block, id_block = block_item
        scores = masked_scores(query_block, id_block)
        top_score = jnp.max(scores, axis=-1, keepdims=True)
        expo_vals = jnp.exp(scores - top_score)
        row_totals = jnp.sum(expo_vals, axis=-1, keepdims=True)
        weights_low = (expo_vals / row_totals).astype(jnp.bfloat16)
        mixed_block = jnp.einsum(
            "hqk,khd->qhd", weights_low, value_heads, preferred_element_type=jnp.float32
        )
        return (mixed_block, top_score + jnp.log(row_totals))

    mixed_heads, log_totals = lax.map(attend, (query_blocks, id_blocks))
    mixed = mixed_heads.reshape(rows_here, D).astype(jnp.bfloat16)
    residual_one = frames + project(mixed, attn_full[3 * D :]) + vectors[6]
    normed_one = layer_norm(residual_one, vectors[0], vectors[1])
    normed_low = normed_one.astype(jnp.bfloat16)
    hidden = project(normed_low, ffn_full[0]) + hidden_bias
    active = jax.nn.gelu(hidden, approximate=False).astype(jnp.bfloat16)
    residual_two = (
        normed_one + jnp.dot(active, ffn_full[1], preferred_element_type=jnp.float32) + vectors[7]
    )
    outputs = layer_norm(residual_two, vectors[2], vectors[3])
    attn_back, ffn_back, small_back = (
        lax.all_gather(attn_weights.astype(jnp.bfloat16), ("dp", "fsdp"), axis=0, tiled=True),
        lax.all_gather(ffn_weights.astype(jnp.bfloat16), ("dp", "fsdp"), axis=1, tiled=True),
        lax.all_gather(small_params.astype(jnp.bfloat16), ("dp", "fsdp"), axis=0, tiled=True),
    )
    vectors_back = small_back[: 8 * D].astype(jnp.float32).reshape(8, D)
    valid = (segment_ids >= 0).astype(jnp.float32)[:, None]
    grad_out = cotangent.astype(jnp.float32) * valid
    _, norm_two_pull = jax.vjp(layer_norm, residual_two, vectors_back[2], vectors_back[3])
    grad_two, gain_two, shift_two = norm_two_pull(grad_out)
    grad_branch = grad_two.astype(jnp.bfloat16)
    down_grad = row_outer(active, grad_branch)
    grad_active = project(grad_branch, ffn_back[1])
    _, gelu_pull = jax.vjp(partial(jax.nn.gelu, approximate=False), hidden)
    (grad_hidden,) = gelu_pull(grad_active)
    grad_hidden_low = grad_hidden.astype(jnp.bfloat16)
    up_grad = row_outer(grad_hidden_low, normed_low)
    ffn_grad = jnp.stack([up_grad, down_grad])
    grad_normed = grad_two + jnp.dot(
        grad_hidden_low, ffn_back[0], preferred_element_type=jnp.float32
    )
    _, norm_one_pull = jax.vjp(layer_norm, residual_one, vectors_back[0], vectors_back[1])
    grad_one, gain_one, shift_one = norm_one_pull(grad_normed)
    grad_proj = grad_one.astype(jnp.bfloat16)
    out_proj_grad = row_outer(grad_proj, mixed)
    grad_mixed = jnp.dot(grad_proj, attn_back[3 * D :], preferred_element_type=jnp.float32).astype(
        jnp.bfloat16
    )
    grad_blocks = grad_mixed.reshape(block_count, block_rows, HEADS, head_dim)

    def attend_back(sums, block_item):
        key_sum, value_sum = sums
        query_block, id_block, log_block, grad_block = block_item
        scores = masked_scores(query_block, id_block)
        weights_attn = jnp.exp(scores - log_block)
        weights_low = weights_attn.astype(jnp.bfloat16)
        value_sum = value_sum + jnp.einsum(
            "hqk,qhd->khd", weights_low, grad_block, preferred_element_type=jnp.float32
        )
        grad_weights = jnp.einsum(
            "qhd,khd->hqk", grad_block, value_heads, preferred_element_type=jnp.float32
        )
        inner_sum = jnp.sum(weights_attn * grad_weights, axis=-1, keepdims=True)
        grad_scores = (weights_attn * (grad_weights - inner_sum)).astype(jnp.bfloat16)
        key_sum = (
            key_sum
            + jnp.einsum(
                "hqk,qhd->khd", grad_scores, query_block, preferred_element_type=jnp.float32
            )
            * score_scale
        )
        query_grad = (
            jnp.einsum("hqk,khd->qhd", grad_scores, key_heads, preferred_element_type=jnp.float32)
            * score_scale
        )
        return ((key_sum, value_sum), query_grad.astype(jnp.bfloat16))

    empty_sum = jnp.zeros((rows_here, HEADS, head_dim), jnp.float32)
    (key_sum, value_sum), query_grads = lax.scan(
        attend_back, (empty_sum, empty_sum), (query_blocks, id_blocks, log_totals, grad_blocks)
    )
    qkv_grad = jnp.concatenate(
        [
            query_grads.reshape(rows_here, D),
            key_sum.reshape(rows_here, D).astype(jnp.bfloat16),
            value_sum.reshape(rows_here, D).astype(jnp.bfloat16),
        ],
        axis=1,
    )
    qkv_weight_grad = row_outer(qkv_grad, features)
    attn_grad = jnp.concatenate([qkv_weight_grad, out_proj_grad], axis=0)
    input_grad = grad_one + jnp.dot(
        qkv_grad, attn_back[: 3 * D], preferred_element_type=jnp.float32
    )
    bias_sums = jnp.sum(qkv_grad, axis=0, dtype=jnp.float32)
    small_grad = jnp.concatenate(
        [
            gain_one,
            shift_one,
            gain_two,
            shift_two,
            bias_sums[:D],
            bias_sums[2 * D :],
            jnp.sum(grad_one, axis=0),
            jnp.sum(grad_two, axis=0),
            jnp.sum(grad_hidden, axis=0),
        ]
    )
    attn_sum, ffn_sum, small_sum = (
        lax.psum_scatter(attn_grad, ("dp", "fsdp"), scatter_dimension=0, tiled=True),
        lax.psum_scatter(ffn_grad, ("dp", "fsdp"), scatter_dimension=1, tiled=True),
        lax.psum_scatter(small_grad, ("dp", "fsdp"), scatter_dimension=0, tiled=True),
    )
    attn_new, attn_first_new, attn_second_new, attn_ema_new = adam_step(
        attn_weights, attn_sum, attn_first, attn_second, attn_ema, 0.01, 0.05
    )
    ffn_new, ffn_first_new, ffn_second_new, ffn_ema_new = adam_step(
        ffn_weights, ffn_sum, ffn_first, ffn_second, ffn_ema, 0.01, 0.05
    )
    small_new, small_first_new, small_second_new, small_ema_new = adam_step(
        small_params, small_sum, small_first, small_second, small_ema, 0.0, 0.3
    )
    return (
        outputs.astype(jnp.bfloat16),
        input_grad,
        attn_new,
        ffn_new,
        small_new,
        attn_first_new,
        ffn_first_new,
        small_first_new,
        attn_second_new,
        ffn_second_new,
        small_second_new,
        attn_ema_new,
        ffn_ema_new,
        small_ema_new,
    )


def solution(mesh):
    in_specs = (
        P(("dp", "fsdp"), None),
        P(("dp", "fsdp"), None),
        P(("dp", "fsdp")),
        P(("dp", "fsdp"), None),
        P(None, ("dp", "fsdp"), None),
        P(("dp", "fsdp")),
        P(("dp", "fsdp"), None),
        P(None, ("dp", "fsdp"), None),
        P(("dp", "fsdp")),
        P(("dp", "fsdp"), None),
        P(None, ("dp", "fsdp"), None),
        P(("dp", "fsdp")),
        P(("dp", "fsdp"), None),
        P(None, ("dp", "fsdp"), None),
        P(("dp", "fsdp")),
    )
    out_specs = (
        P(("dp", "fsdp"), None),
        P(("dp", "fsdp"), None),
        P(("dp", "fsdp"), None),
        P(None, ("dp", "fsdp"), None),
        P(("dp", "fsdp")),
        P(("dp", "fsdp"), None),
        P(None, ("dp", "fsdp"), None),
        P(("dp", "fsdp")),
        P(("dp", "fsdp"), None),
        P(None, ("dp", "fsdp"), None),
        P(("dp", "fsdp")),
        P(("dp", "fsdp"), None),
        P(None, ("dp", "fsdp"), None),
        P(("dp", "fsdp")),
    )
    return jax.shard_map(local, mesh=mesh, in_specs=in_specs, out_specs=out_specs, check_vma=False)
```

profile of v0, /device:TPU:0, one launch (start us, length us, event | category | flops | bytes accessed | tf_op | source)
XLA Modules:
  0.0 819.6 jit_solution(2694873453621263957)
XLA Ops:
  16.8 42.5 %all-reduce = bf16[9216]{0:T(1024)(128)(2,1)S(1)} all-reduce(bf16[9216]{0:T(1024)(128)(2,1)S(1)} %dynamic-update-slice), channel_id=1, replica_groups=mesh['dp'=8,'fsdp'=4] {'dp','fsdp'}, use_global_device_ids=true, to_apply=%add | all-reduce | flops 9216 | bytes 36864
  61.1 16.8 %all-gather.3.cloned.1.call-done = bf16[3072,768]{1,0:T(8,128)(2,1)} async-done(((bf16[96,768]{1,0:T(8,128)(2,1)}), bf16[3072,768]{1,0:T(8,128)(2,1)}) %all-gather.3.cloned.1.call-update) | async-done | bytes 4718608 | tf_op jit(solution)/shard_map/all_gather | solution.py:64
  92.2 70.9 %while.27 = (s32[]{:T(128)}, bf16[2,512,12,64]{1,3,2,0:T(8,128)(2,1)}, f32[2,12,512,1]{2,1,3,0:T(8,128)S(1)}, s32[2,512]{1,0:T(2,128)S(1)}, s32[1024]{0:T(1024)S...) while((s32[]{:T(128)}, ...), condition=%wide.region_3.4_spmd, body=%wide.region_0.3_spmd.sunk | while | flops 1686628352 | bytes 190286000 | solution.py:99
  92.6 10.6 %fusion.111 = (f32[12,512]{1,0:T(8,128)S(1)}, f32[12,512,1024]{2,1,0:T(8,128)}) fusion(pred[512,1024]{1,0:T(8,128)(4,1)S(1)} %broadcast_compare_fusion.4, bf16[1024,12,64]{0,2,1:T(8,128)(2,1)S(1)} %get-tuple-element.489, bf16[2,512,12,64]{1,3,2,0:T(8,128)(2,1)S(1)} %get-tuple-element.488, s32[]{:T(128)S(6)} %copy.75), kind=kOutput, calls=%fused_computation.3.clone.1 | convolution fusion | flops 824174592 | bytes 28073988 | tf_op jit(solution)/shard_map/while/body/eval_jaxpr/qhd,khd->hqk/dot_general | solution.py:81
  103.2 12.6 %fusion.112 = f32[12,512]{1,0:T(8,128)S(1)} fusion(f32[12,512,1024]{2,1,0:T(8,128)} %get-tuple-element.450, f32[12,512]{1,0:T(8,128)S(1)} %get-tuple-element.451, pred[512,1024]{1,0:T(8,128)(4,1)S(1)} %broadcast_compare_fusion.4), kind=kLoop, calls=%fused_computation.4.clone.1 | loop fusion | flops 25159680 | bytes 25739264 | tf_op jit(solution)/shard_map/while/body/eval_jaxpr/reduce_sum | solution.py:92
  118.9 8.5 %bitcast_dynamic-update-slice_fusion.4 = bf16[2,512,12,64]{1,3,2,0:T(8,128)(2,1)} fusion(bf16[2,512,12,64]{1,3,2,0:T(8,128)(2,1)} %get-tuple-element.475, s32[]{:T(128)S(6)} %copy.75, bf16[1024,12,64]{0,2,1:T(8,128)(2,1)S(1)} %copy-done.6, f32[12,512,1024]{2,1,0:T(8,128)S(1)} %copy-done, f32[12,512]{1,0:T(8,128)S(1)} %fusion.112, ...), kind=kOutput, calls=%fused_computation.6.clone.1 | convolution fusion | flops 836763648 | bytes 28884996 | tf_op jit(solution)/shard_map/while/body/eval_jaxpr/hqk,khd->qhd/dot_general | solution.py:94
  127.8 10.8 %fusion.111 = (f32[12,512]{1,0:T(8,128)S(1)}, f32[12,512,1024]{2,1,0:T(8,128)}) fusion(pred[512,1024]{1,0:T(8,128)(4,1)S(1)} %broadcast_compare_fusion.4, bf16[1024,12,64]{0,2,1:T(8,128)(2,1)S(1)} %get-tuple-element.489, bf16[2,512,12,64]{1,3,2,0:T(8,128)(2,1)S(1)} %get-tuple-element.488, s32[]{:T(128)S(6)} %copy.75), kind=kOutput, calls=%fused_computation.3.clone.1 | convolution fusion | flops 824174592 | bytes 28073988 | tf_op jit(solution)/shard_map/while/body/eval_jaxpr/qhd,khd->hqk/dot_general | solution.py:81
  138.6 12.3 %fusion.112 = f32[12,512]{1,0:T(8,128)S(1)} fusion(f32[12,512,1024]{2,1,0:T(8,128)} %get-tuple-element.450, f32[12,512]{1,0:T(8,128)S(1)} %get-tuple-element.451, pred[512,1024]{1,0:T(8,128)(4,1)S(1)} %broadcast_compare_fusion.4), kind=kLoop, calls=%fused_computation.4.clone.1 | loop fusion | flops 25159680 | bytes 25739264 | tf_op jit(solution)/shard_map/while/body/eval_jaxpr/reduce_sum | solution.py:92
  154.4 8.5 %bitcast_dynamic-update-slice_fusion.4 = bf16[2,512,12,64]{1,3,2,0:T(8,128)(2,1)} fusion(bf16[2,512,12,64]{1,3,2,0:T(8,128)(2,1)} %get-tuple-element.475, s32[]{:T(128)S(6)} %copy.75, bf16[1024,12,64]{0,2,1:T(8,128)(2,1)S(1)} %copy-done.6, f32[12,512,1024]{2,1,0:T(8,128)S(1)} %copy-done, f32[12,512]{1,0:T(8,128)S(1)} %fusion.112, ...), kind=kOutput, calls=%fused_computation.6.clone.1 | convolution fusion | flops 836763648 | bytes 28884996 | tf_op jit(solution)/shard_map/while/body/eval_jaxpr/hqk,khd->qhd/dot_general | solution.py:94
  172.2 38.2 %multiply_convert_fusion.2 = (bf16[1024,3072]{1,0:T(8,128)(2,1)}, f32[1024,3072]{1,0:T(8,128)}, f32[1024,3072]{1,0:T(8,128)}) fusion(f32[3072]{0:T(1024)S(1)} %copy-done.51, bf16[2,3072,768]{2,1,0:T(8,128)(2,1)} %all-gather.5.cloned.1.call-done, f32[1024,768]{0,1:T(8,128)S(1)} %get-tuple-element.332, f32[768]{0:T(1024)S(1)} %copy-done.53, ...), kind=kOutput, calls=%fused_computation.50 | convolution fusion | flops 5043388416 | bytes 39348224 | tf_op jit(solution)/shard_map/dot_general | solution.py:20
  210.4 8.7 %fusion.75 = (f32[1024]{0:T(1024)S(1)}, f32[1024,768]{0,1:T(8,128)S(1)}) fusion(f32[768]{0:T(1024)S(1)} %copy-done.55, bf16[1024,3072]{1,0:T(8,128)(2,1)} %get-tuple-element.316, bf16[2,3072,768]{2,1,0:T(8,128)(2,1)S(1)} %copy-done.62, f32[768]{0:T(1024)S(1)} %copy-done.53, f32[768]{0:T(1024)S(1)} %copy-done.40, f32[1024]{0:T(1024)S(1)} %fusion.61, ...), kind=kOutput, calls=%fused_computation.152 | convolution fusion | flops 4837342208 | bytes 17326080 | tf_op jit(solution)/shard_map/dot_general | solution.py:107
  225.4 18.7 %fusion.76 = (f32[3072]{0:T(1024)}, bf16[1024,3072]{1,0:T(8,128)(2,1)}) fusion(f32[1024,3072]{1,0:T(8,128)} %get-tuple-element.317, bf16[2,3072,768]{2,1,0:T(8,128)(2,1)} %all-gather.5.cloned.1.call-done, f32[1024,768]{0,1:T(8,128)S(1)} %get-tuple-element.315, f32[1024]{0:T(1024)S(1)} %negate_multiply_fusion.2, f32[1024,3072]{1,0:T(8,128)} %get-tuple-element.333, ...), kind=kOutput, calls=%fused_computation.153 | convolution fusion | flops 4883739648 | bytes 39350272 | tf_op jit(solution)/shard_map/dot_general | solution.py:20
  244.1 10.9 %multiply_reduce_fusion.2 = (f32[768]{0:T(1024)}, f32[1024]{0:T(1024)S(1)}, f32[768]{0:T(1024)}, f32[1024,768]{0,1:T(8,128)S(1)}) fusion(f32[1024,768]{0,1:T(8,128)} %copy-done.11, f32[1024]{0:T(1024)S(1)} %fusion.61, f32[1024]{0:T(1024)S(1)} %broadcast_multiply_fusion.1, f32[768]{0:T(1024)S(1)} %copy-done.40, ...), kind=kOutput, calls=%fused_computation.79 | convolution fusion | flops 4839699456 | bytes 20472832 | tf_op jit(solution)/shard_map/dot_general | solution.py:128
  268.2 167.8 %while.28 = (s32[]{:T(128)}, f32[1024,12,64]{0,2,1:T(8,128)}, f32[1024,12,64]{0,2,1:T(8,128)}, bf16[2,512,12,64]{1,3,2,0:T(8,128)(2,1)}, bf16[2,512,12,64]{1,3,2...) while((s32[]{:T(128)}, f32[1024,12,64]{0,2,1:T(8,128)}, ...), condition=%wide.region_14.15_spmd.clone, body=%wide.region_12.14_spmd.clone.sunk | while | flops 4126140416 | bytes 224848080 | solution.py:168
  269.0 11.4 %fusion.122 = f32[12,512,1024]{2,1,0:T(8,128)} fusion(bf16[1024,12,64]{0,2,1:T(8,128)(2,1)S(1)} %get-tuple-element.525, bf16[2,512,12,64]{1,3,2,0:T(8,128)(2,1)} %get-tuple-element.522, s32[]{:T(128)S(6)} %copy.85), kind=kOutput, calls=%fused_computation.32.clone.1 | convolution fusion | flops 805306368 | bytes 27525124 | tf_op jit(solution)/shard_map/while/body/eval_jaxpr/qhd,khd->hqk/dot_general | solution.py:81
  280.4 13.4 %bitcast_add_fusion.5 = f32[1024,12,64]{0,2,1:T(8,128)} fusion(f32[1024,12,64]{0,2,1:T(8,128)} %get-tuple-element.507, f32[12,512,1024]{2,1,0:T(8,128)} %fusion.122, f32[12,512]{1,0:T(8,128)S(1)} %dynamic-slice_bitcast_fusion.2, pred[512,1024]{1,0:T(8,128)(4,1)S(1)} %broadcast_compare_fusion.5, pred[]{:T(512)S(6)} %compare.3, ...), kind=kOutput, calls=%fused_computation.22.clone.1 | convolution fusion | flops 832045056 | bytes 32800772 | tf_op jit(solution)/shard_map/while/body/eval_jaxpr/hqk,qhd->khd/dot_general | solution.py:146
  293.8 18.1 %multiply_reduce_fusion.8 = (f32[12,512]{1,0:T(8,128)S(1)}, f32[12,512,1024]{2,1,0:T(8,128)}) fusion(f32[12,512,1024]{2,1,0:T(8,128)} %fusion.122, f32[12,512]{1,0:T(8,128)S(1)} %dynamic-slice_bitcast_fusion.2, pred[512,1024]{1,0:T(8,128)(4,1)S(1)} %broadcast_compare_fusion.5, bf16[1024,12,64]{0,2,1:T(8,128)(2,1)} %get-tuple-element.528, ...), kind=kOutput, calls=%fused_computation.17.clone.1 | convolution fusion | flops 836757504 | bytes 53264388 | tf_op jit(solution)/shard_map/while/body/eval_jaxpr/qhd,khd->hqk/dot_general | solution.py:149
  311.9 21.2 %multiply_convert_fusion.4 = bf16[12,512,1024]{2,1,0:T(8,128)(2,1)} fusion(f32[12,512,1024]{2,1,0:T(8,128)} %get-tuple-element.463, f32[12,512,1024]{2,1,0:T(8,128)} %fusion.122, f32[12,512]{1,0:T(8,128)S(1)} %get-tuple-element.464, f32[12,512]{1,0:T(8,128)S(1)} %dynamic-slice_bitcast_fusion.2, pred[512,1024]{1,0:T(8,128)(4,1)S(1)} %broadcast_compare_fusion.5), kind=kLoop, calls=%fused_computation.16.clone.1 | loop fusion | flops 37748736 | bytes 63488000 | tf_op jit(solution)/shard_map/while/body/eval_jaxpr/convert_element_type | solution.py:153
  333.2 9.5 %fusion.123 = bf16[2,512,12,64]{1,3,2,0:T(8,128)(2,1)} fusion(bf16[2,512,12,64]{1,3,2,0:T(8,128)(2,1)} %get-tuple-element.508, s32[]{:T(128)S(6)} %copy.85, bf16[12,512,1024]{2,1,0:T(8,128)(2,1)} %multiply_convert_fusion.4, bf16[1024,12,64]{0,2,1:T(8,128)(2,1)S(1)} %get-tuple-element.525), kind=kOutput, calls=%fused_computation.26.clone.1 | convolution fusion | flops 806092800 | bytes 14942212 | tf_op jit(solution)/shard_map/while/body/eval_jaxpr/hqk,khd->qhd/dot_general | solution.py:162
  342.7 8.6 %bitcast_add_fusion.4 = f32[1024,12,64]{0,2,1:T(8,128)} fusion(f32[1024,12,64]{0,2,1:T(8,128)} %get-tuple-element.506, bf16[12,512,1024]{2,1,0:T(8,128)(2,1)} %multiply_convert_fusion.4, pred[]{:T(512)S(6)} %compare.3, bf16[2,512,12,64]{1,3,2,0:T(8,128)(2,1)S(1)} %copy-done.5, s32[]{:T(128)S(6)} %copy.85), kind=kOutput, calls=%fused_computation.23.clone.1 | convolution fusion | flops 807665664 | bytes 19660804 | tf_op jit(solution)/shard_map/while/body/eval_jaxpr/hqk,qhd->khd/dot_general | solution.py:156
  351.7 11.4 %fusion.122 = f32[12,512,1024]{2,1,0:T(8,128)} fusion(bf16[1024,12,64]{0,2,1:T(8,128)(2,1)S(1)} %get-tuple-element.525, bf16[2,512,12,64]{1,3,2,0:T(8,128)(2,1)} %get-tuple-element.522, s32[]{:T(128)S(6)} %copy.85), kind=kOutput, calls=%fused_computation.32.clone.1 | convolution fusion | flops 805306368 | bytes 27525124 | tf_op jit(solution)/shard_map/while/body/eval_jaxpr/qhd,khd->hqk/dot_general | solution.py:81
  363.1 14.3 %bitcast_add_fusion.5 = f32[1024,12,64]{0,2,1:T(8,128)} fusion(f32[1024,12,64]{0,2,1:T(8,128)} %get-tuple-element.507, f32[12,512,1024]{2,1,0:T(8,128)} %fusion.122, f32[12,512]{1,0:T(8,128)S(1)} %dynamic-slice_bitcast_fusion.2, pred[512,1024]{1,0:T(8,128)(4,1)S(1)} %broadcast_compare_fusion.5, pred[]{:T(512)S(6)} %compare.3, ...), kind=kOutput, calls=%fused_computation.22.clone.1 | convolution fusion | flops 832045056 | bytes 32800772 | tf_op jit(solution)/shard_map/while/body/eval_jaxpr/hqk,qhd->khd/dot_general | solution.py:146
  377.5 18.1 %multiply_reduce_fusion.8 = (f32[12,512]{1,0:T(8,128)S(1)}, f32[12,512,1024]{2,1,0:T(8,128)}) fusion(f32[12,512,1024]{2,1,0:T(8,128)} %fusion.122, f32[12,512]{1,0:T(8,128)S(1)} %dynamic-slice_bitcast_fusion.2, pred[512,1024]{1,0:T(8,128)(4,1)S(1)} %broadcast_compare_fusion.5, bf16[1024,12,64]{0,2,1:T(8,128)(2,1)} %get-tuple-element.528, ...), kind=kOutput, calls=%fused_computation.17.clone.1 | convolution fusion | flops 836757504 | bytes 53264388 | tf_op jit(solution)/shard_map/while/body/eval_jaxpr/qhd,khd->hqk/dot_general | solution.py:149
  395.6 21.2 %multiply_convert_fusion.4 = bf16[12,512,1024]{2,1,0:T(8,128)(2,1)} fusion(f32[12,512,1024]{2,1,0:T(8,128)} %get-tuple-element.463, f32[12,512,1024]{2,1,0:T(8,128)} %fusion.122, f32[12,512]{1,0:T(8,128)S(1)} %get-tuple-element.464, f32[12,512]{1,0:T(8,128)S(1)} %dynamic-slice_bitcast_fusion.2, pred[512,1024]{1,0:T(8,128)(4,1)S(1)} %broadcast_compare_fusion.5), kind=kLoop, calls=%fused_computation.16.clone.1 | loop fusion | flops 37748736 | bytes 63488000 | tf_op jit(solution)/shard_map/while/body/eval_jaxpr/convert_element_type | solution.py:153
  416.8 9.5 %fusion.123 = bf16[2,512,12,64]{1,3,2,0:T(8,128)(2,1)} fusion(bf16[2,512,12,64]{1,3,2,0:T(8,128)(2,1)} %get-tuple-element.508, s32[]{:T(128)S(6)} %copy.85, bf16[12,512,1024]{2,1,0:T(8,128)(2,1)} %multiply_convert_fusion.4, bf16[1024,12,64]{0,2,1:T(8,128)(2,1)S(1)} %get-tuple-element.525), kind=kOutput, calls=%fused_computation.26.clone.1 | convolution fusion | flops 806092800 | bytes 14942212 | tf_op jit(solution)/shard_map/while/body/eval_jaxpr/hqk,khd->qhd/dot_general | solution.py:162
  426.3 9.5 %bitcast_add_fusion.4 = f32[1024,12,64]{0,2,1:T(8,128)} fusion(f32[1024,12,64]{0,2,1:T(8,128)} %get-tuple-element.506, bf16[12,512,1024]{2,1,0:T(8,128)(2,1)} %multiply_convert_fusion.4, pred[]{:T(512)S(6)} %compare.3, bf16[2,512,12,64]{1,3,2,0:T(8,128)(2,1)S(1)} %copy-done.5, s32[]{:T(128)S(6)} %copy.85), kind=kOutput, calls=%fused_computation.23.clone.1 | convolution fusion | flops 807665664 | bytes 19660804 | tf_op jit(solution)/shard_map/while/body/eval_jaxpr/hqk,qhd->khd/dot_general | solution.py:156
  444.1 9.2 %fusion.64 = f32[2304,768]{1,0:T(8,128)} fusion(bf16[1024,768]{1,0:T(8,128)(2,1)S(1)} %copy-done.22, bf16[1024,768]{0,1:T(8,128)(2,1)S(1)} %bitcast.146, bf16[1024,768]{0,1:T(8,128)(2,1)S(1)} %bitcast.143, bf16[1024,768]{0,1:T(8,128)(2,1)S(1)} %bitcast.140), kind=kOutput, calls=%fused_computation.147 | convolution fusion | flops 3638034432 | bytes 13369344 | tf_op jit(solution)/shard_map/dot_general | solution.py:26
  470.0 8.1 convolution_bitcast_fusion.1
  485.9 10.5 %add_add_fusion.4 = f32[1024,768]{0,1:T(8,128)} fusion(f32[1024,768]{0,1:T(8,128)} %copy-done.14, bf16[3072,768]{1,0:T(8,128)(2,1)} %all-gather.3.cloned.1.call-done, f32[1024]{0:T(1024)S(1)} %copy-done.47, bf16[1024,768]{0,1:T(8,128)(2,1)} %bitcast.147, bf16[1024,768]{0,1:T(8,128)(2,1)} %bitcast.144, bf16[1024,768]{0,1:T(8,128)(2,1)} %bitcast.141), kind=kOutput, calls=%fused_computation.96 | convolution fusion | flops 3639607296 | bytes 14553088 | tf_op jit(solution)/shard_map/dot_general | solution.py:181
  506.7 43.2 %all-reduce.1 = f32[9216]{0:T(1024)S(1)} all-reduce(f32[9216]{0:T(1024)S(1)} %constant_dynamic-update-slice_fusion), channel_id=4, replica_groups=mesh['dp'=8,'fsdp'=4] {'dp','fsdp'}, use_global_device_ids=true, to_apply=%region_25.26.clone | all-reduce | flops 9216 | bytes 73728
  550.6 47.4 %reduce-scatter.3.cloned.1.call-done = f32[96,768]{1,0:T(8,128)} async-done(((f32[3072,768]{1,0:T(8,128)}), f32[96,768]{1,0:T(8,128)}) %reduce-scatter.3.cloned.1.call-update) | async-done | bytes 294928 | tf_op jit(solution)/shard_map/reduce_scatter | solution.py:199
  600.4 209.0 %reduce-scatter.5.cloned.1.call-done = f32[2,96,768]{2,1,0:T(8,128)} async-done(((f32[2,3072,768]{2,1,0:T(8,128)}), f32[2,96,768]{2,1,0:T(8,128)}) %reduce-scatter.5.cloned.1.call-update) | async-done | bytes 589840 | tf_op jit(solution)/shard_map/reduce_scatter | solution.py:200
  (224 shorter events, 111.0 us)
Async XLA Ops:
  7.2 70.7 %all-gather.3.cloned.1.call-start = ((), (), s32[]{:S(2)}) async-start(), calls=%async_computation.2 | async-start | bytes 4866048 | tf_op jit(solution)/shard_map/all_gather | solution.py:64
  9.0 163.2 %all-gather.5.cloned.1.call-start = ((), (), s32[]{:S(2)}) async-start(), calls=%async_computation.3 | async-start | bytes 9732096 | tf_op jit(solution)/shard_map/all_gather | solution.py:65
  10.9 587.1 %reduce-scatter.3.cloned.1.call-start = ((), (), s32[]{:S(2)}) async-start(), calls=%async_computation.4 | async-start | bytes 9732096 | tf_op jit(solution)/shard_map/reduce_scatter | solution.py:199
  12.4 46.9 %copy-start.27 = (s32[1024]{0:T(1024)S(1)}, s32[1024]{0:T(1024)}, u32[]{:S(2)}) copy-start(s32[1024]{0:T(1024)} %param.21) | copy-start | bytes 12292
  92.5 23.2 %copy-start.6 = (bf16[1024,12,64]{0,2,1:T(8,128)(2,1)S(1)}, bf16[1024,12,64]{0,2,1:T(8,128)(2,1)}, u32[]{:S(2)}) copy-start(bf16[1024,12,64]{0,2,1:T(8,128)(2,1)} %get-tuple-element.490) | copy-start | bytes 4718596 | tf_op jit(solution)/shard_map/while
  103.2 15.7 %copy-start = (f32[12,512,1024]{2,1,0:T(8,128)S(1)}, f32[12,512,1024]{2,1,0:T(8,128)}, u32[]{:S(2)}) copy-start(f32[12,512,1024]{2,1,0:T(8,128)} %get-tuple-element.450) | copy-start | bytes 75497472 | tf_op jit(solution)/shard_map/while
  127.8 23.1 %copy-start.6 = (bf16[1024,12,64]{0,2,1:T(8,128)(2,1)S(1)}, bf16[1024,12,64]{0,2,1:T(8,128)(2,1)}, u32[]{:S(2)}) copy-start(bf16[1024,12,64]{0,2,1:T(8,128)(2,1)} %get-tuple-element.490) | copy-start | bytes 4718596 | tf_op jit(solution)/shard_map/while
  138.6 15.8 %copy-start = (f32[12,512,1024]{2,1,0:T(8,128)S(1)}, f32[12,512,1024]{2,1,0:T(8,128)}, u32[]{:S(2)}) copy-start(f32[12,512,1024]{2,1,0:T(8,128)} %get-tuple-element.450) | copy-start | bytes 75497472 | tf_op jit(solution)/shard_map/while
  171.1 39.3 %copy-start.11 = (f32[1024,768]{0,1:T(8,128)}, f32[1024,768]{0,1:T(8,128)S(1)}, u32[]{:S(2)}) copy-start(f32[1024,768]{0,1:T(8,128)S(1)} %get-tuple-element.332) | copy-start | bytes 9437188
  171.2 83.9 %copy-start.35 = (f32[1024]{0:T(1024)}, f32[1024]{0:T(1024)S(1)}, u32[]{:S(2)}) copy-start(f32[1024]{0:T(1024)S(1)} %broadcast_multiply_fusion.1) | copy-start | bytes 12292
  172.2 82.9 %copy-start.44 = (f32[1024]{0:T(1024)}, f32[1024]{0:T(1024)S(1)}, u32[]{:S(2)}) copy-start(f32[1024]{0:T(1024)S(1)} %fusion.61) | copy-start | bytes 12292
  172.2 38.2 %copy-start.55 = (f32[768]{0:T(1024)S(1)}, f32[768]{0:T(1024)}, u32[]{:S(2)}) copy-start(f32[768]{0:T(1024)} %get-tuple-element.325) | copy-start | bytes 9220
  172.2 38.2 %copy-start.62 = (bf16[2,3072,768]{2,1,0:T(8,128)(2,1)S(1)}, bf16[2,3072,768]{2,1,0:T(8,128)(2,1)}, u32[]{:S(2)}) copy-start(bf16[2,3072,768]{2,1,0:T(8,128)(2,1)} %all-gather.5.cloned.1.call-done) | copy-start | bytes 28311556
  225.4 18.7 %copy-start.9 = (f32[1024,768]{0,1:T(8,128)}, f32[1024,768]{0,1:T(8,128)S(1)}, u32[]{:S(2)}) copy-start(f32[1024,768]{0,1:T(8,128)S(1)} %get-tuple-element.315) | copy-start | bytes 9437188
  225.4 18.7 %copy-start.42 = (f32[1024]{0:T(1024)}, f32[1024]{0:T(1024)S(1)}, u32[]{:S(2)}) copy-start(f32[1024]{0:T(1024)S(1)} %negate_multiply_fusion.2) | copy-start | bytes 12292
  244.1 10.9 %copy-start.38 = (f32[1024]{0:T(1024)S(1)}, f32[1024]{0:T(1024)}, u32[]{:S(2)}) copy-start(f32[1024]{0:T(1024)} %copy-done.37) | copy-start | bytes 12292
  244.1 11.0 %copy-start.12 = (f32[1024,768]{0,1:T(8,128)S(1)}, f32[1024,768]{0,1:T(8,128)}, u32[]{:S(2)}) copy-start(f32[1024,768]{0,1:T(8,128)} %copy-done.11) | copy-start | bytes 9437188
  269.0 11.4 %copy-start.7 = (bf16[2,512,12,64]{1,3,2,0:T(8,128)(2,1)S(1)}, bf16[2,512,12,64]{1,3,2,0:T(8,128)(2,1)}, u32[]{:S(2)}) copy-start(bf16[2,512,12,64]{1,3,2,0:T(8,128)(2,1)} %get-tuple-element.527) | copy-start | bytes 4718596 | tf_op jit(solution)/shard_map/while
  333.2 9.5 %copy-start.5 = (bf16[2,512,12,64]{1,3,2,0:T(8,128)(2,1)S(1)}, bf16[2,512,12,64]{1,3,2,0:T(8,128)(2,1)}, u32[]{:S(2)}) copy-start(bf16[2,512,12,64]{1,3,2,0:T(8,128)(2,1)} %get-tuple-element.522) | copy-start | bytes 4718596 | tf_op jit(solution)/shard_map/while
  351.7 11.4 %copy-start.7 = (bf16[2,512,12,64]{1,3,2,0:T(8,128)(2,1)S(1)}, bf16[2,512,12,64]{1,3,2,0:T(8,128)(2,1)}, u32[]{:S(2)}) copy-start(bf16[2,512,12,64]{1,3,2,0:T(8,128)(2,1)} %get-tuple-element.527) | copy-start | bytes 4718596 | tf_op jit(solution)/shard_map/while
  416.8 9.5 %copy-start.5 = (bf16[2,512,12,64]{1,3,2,0:T(8,128)(2,1)S(1)}, bf16[2,512,12,64]{1,3,2,0:T(8,128)(2,1)}, u32[]{:S(2)}) copy-start(bf16[2,512,12,64]{1,3,2,0:T(8,128)(2,1)} %get-tuple-element.522) | copy-start | bytes 4718596 | tf_op jit(solution)/shard_map/while
  444.1 9.2 %copy-start.19 = (f32[768,768]{1,0:T(8,128)S(1)}, f32[768,768]{1,0:T(8,128)}, u32[]{:S(2)}) copy-start(f32[768,768]{1,0:T(8,128)} %fusion.58) | copy-start | bytes 7077892
  460.6 9.3 %copy-start.36 = (f32[1024]{0:T(1024)S(1)}, f32[1024]{0:T(1024)}, u32[]{:S(2)}) copy-start(f32[1024]{0:T(1024)} %copy-done.35) | copy-start | bytes 12292
  460.6 9.3 %copy-start.41 = (f32[768]{0:T(1024)S(1)}, f32[768]{0:T(1024)}, u32[]{:S(2)}) copy-start(f32[768]{0:T(1024)} %get-tuple-element.327) | copy-start | bytes 9220
  460.6 9.3 %copy-start.45 = (f32[1024]{0:T(1024)S(1)}, f32[1024]{0:T(1024)}, u32[]{:S(2)}) copy-start(f32[1024]{0:T(1024)} %copy-done.44) | copy-start | bytes 12292
  460.7 9.3 %copy-start.54 = (f32[768]{0:T(1024)S(1)}, f32[768]{0:T(1024)}, u32[]{:S(2)}) copy-start(f32[768]{0:T(1024)} %get-tuple-element.326) | copy-start | bytes 9220
  460.7 348.8 %reduce-scatter.5.cloned.1.call-start = ((), (), s32[]{:S(2)}) async-start(), calls=%async_computation.5 | async-start | bytes 19464192 | tf_op jit(solution)/shard_map/reduce_scatter | solution.py:200
  506.0 43.9 %copy-start.52 = (f32[288]{0:T(512)S(1)}, f32[288]{0:T(512)}, u32[]{:S(2)}) copy-start(f32[288]{0:T(512)} %param.24) | copy-start | bytes 3460
  506.0 43.9 %copy-start.59 = (f32[288]{0:T(512)S(1)}, f32[288]{0:T(512)}, u32[]{:S(2)}) copy-start(f32[288]{0:T(512)} %param.33) | copy-start | bytes 3460
  506.0 43.9 %copy-start.60 = (f32[288]{0:T(512)S(1)}, f32[288]{0:T(512)}, u32[]{:S(2)}) copy-start(f32[288]{0:T(512)} %param.27) | copy-start | bytes 3460
  506.0 43.9 %copy-start.61 = (f32[288]{0:T(512)S(1)}, f32[288]{0:T(512)}, u32[]{:S(2)}) copy-start(f32[288]{0:T(512)} %param.30) | copy-start | bytes 3460
  506.0 92.0 %copy-start.26 = (f32[96,768]{1,0:T(8,128)S(1)}, f32[96,768]{1,0:T(8,128)}, u32[]{:S(2)}) copy-start(f32[96,768]{1,0:T(8,128)} %param.22) | copy-start | bytes 884740
  (39 other events, 123.6 us)
Sparse Core Ops, SparseCore 0:
  11.5 66.3 all-gather.2
  81.4 80.9 all-gather.4
  460.7 137.2 reduce-scatter.2
  605.4 203.9 reduce-scatter.4
where the time goes:
time: 829 us; the launch traced here: 820 us
  matrix products  292 us (35%)
  waiting for transfers between devices  273 us (33%)
  other arithmetic  108 us (13%)
  blocking collectives  85.7 us (10%)
  local copies, waits for them, and re-layouts  44.2 us (5%)
  between operations  14.9 us (2%)
    reduce_scatter x1, waiting for transfers between devices, local(): lax.psum_scatter(ffn_grad, ('dp', 'fsdp'), scatter_dimension=1, tiled=True)  209 us
    unnamed x2, blocking collectives  85.7 us
    dot_general x6, matrix products, project(): lax.dot_general(left_arg, weight_mat, (((1,), (1,)), ((), ())), preferred...  69.4 us
    reduce_scatter x1, waiting for transfers between devices, local(): lax.psum_scatter(attn_grad, ('dp', 'fsdp'), scatter_dimension=0, tiled=True)  47.4 us
    dot_general x4, matrix products, masked_scores(): jnp.einsum('qhd,khd->hqk', query_block, key_heads, preferred_element_type...  44.2 us
    convert_element_type x2, other arithmetic, attend_back(): (weights_attn * (grad_weights - inner_sum)).astype(jnp.bfloat16)  42.5 us
    dot_general x2, matrix products, attend_back(): jnp.einsum('qhd,khd->hqk', grad_block, value_heads, preferred_element_typ...  36.2 us
    dot_general x2, matrix products, attend_back(): jnp.einsum('hqk,qhd->khd', weights_low, grad_block, preferred_element_typ...  27.8 us
  transfers between devices with their start and end apart: 4, of which 3 were waited for; matrix products, arithmetic and copies ran while one was open for 17% of the time, Pallas kernels for 0%

commit v1 on v0

v1 whole, which is shorter than its diff:
```python
from functools import partial

import jax
import jax.numpy as jnp
from jax import lax
from jax.experimental import pallas as pl
from jax.experimental.pallas import tpu as pltpu
from jax.sharding import PartitionSpec as P

D = 768
HEADS = 12
HD = D // HEADS
STEP = 10
LOG2E = 1.4426950408889634
INV_SQRT2 = 0.7071067811865476
INV_SQRT2PI = 0.3989422804014327
BIG = 2.0**30
VMEM_LIMIT = 60 * 1024 * 1024

bf = jnp.bfloat16
f32 = jnp.float32
TN = (((0,), (0,)), ((), ()))
NN = (((1,), (0,)), ((), ()))
NT = (((1,), (1,)), ((), ()))


def dot(left, right, dims):
    return lax.dot_general(left, right, dims, preferred_element_type=f32)


def rows_at(i, size):
    return pl.ds(pl.multiple_of(i * size, size), size)


def column(row):
    return jnp.transpose(jnp.broadcast_to(row, (128, row.shape[1])))


def widen(col, width):
    return jnp.concatenate([col] * (width // 128), axis=1) if width > 128 else col


def lane_fold(x):
    total = x[:, :128]
    for i in range(1, x.shape[1] // 128):
        total = total + x[:, 128 * i : 128 * (i + 1)]
    return total


def fold_row(part):
    return jnp.sum(jnp.transpose(part), axis=0, keepdims=True)


def segment_rows(seg):
    ids = lax.broadcasted_iota(jnp.int32, (16, seg.shape[1]), 0) - 1
    same = jnp.where(ids == seg, 1.0, 0.0)
    return ((same - 1.0) * BIG).astype(bf), same.astype(bf)


def forward_kernel(x_ref, seg_ref, w_ref, sm_ref, qkv_ref, o_ref, l_ref):
    t = x_ref.shape[0]
    block = 256

    def project_block(i, _):
        rows = rows_at(i, block)
        sec = i // (D // block)
        off = i - sec * (D // block)
        bias = sm_ref[:, pl.ds(pl.multiple_of((4 + sec // 2) * D + off * block, block), block)]
        keep = jnp.where(sec == 1, 0.0, 1.0)
        col = column(bias.astype(f32) * keep)
        qkv_ref[rows, :] = (dot(w_ref[rows, :], x_ref[...], NT) + widen(col, t)).astype(bf)
        return 0

    lax.fori_loop(0, 3 * D // block, project_block, 0)
    q_rows, k_rows = segment_rows(seg_ref[...])

    def head(h, _):
        rows = rows_at(h, HD)
        q = qkv_ref[rows, :] * bf(0.125)
        k = qkv_ref[pl.ds(pl.multiple_of(D + h * HD, HD), HD), :]
        v = qkv_ref[pl.ds(pl.multiple_of(2 * D + h * HD, HD), HD), :]
        s = dot(jnp.concatenate([k, k_rows], 0), jnp.concatenate([q, q_rows], 0), TN)
        top = jnp.max(s, axis=0, keepdims=True)
        e = jnp.exp2((s - top) * LOG2E)
        total = jnp.sum(e, axis=0, keepdims=True)
        o_ref[rows, :] = (dot(v, e.astype(bf), NN) * (1.0 / total)).astype(bf)
        l_ref[h] = top + jnp.log(total)
        return 0

    lax.fori_loop(0, HEADS, head, 0)


def gelu_both(h):
    cdf = 0.5 + 0.5 * lax.erf(h * INV_SQRT2)
    pdf = jnp.exp(h * h * -0.5) * INV_SQRT2PI
    return h * cdf, cdf + h * pdf


VECS = (0, 1, 2, 3, 6, 7)


def middle_kernel(
    x_ref, o_ref, cot_ref, seg_ref, wo_ref, w1_ref, w2_ref, sm_ref,
    out_ref, dr1_ref, do_ref, dwo_ref, dw1_ref, dw2_ref, sg_ref,
    a1_ref, xh_ref, act_ref, gp_ref, rs_ref, low_ref, df_ref, vec_ref, part_ref,
):
    t = x_ref.shape[0]
    ff = w1_ref.shape[0]
    block, lanes = 256, 256
    for n, i in enumerate(VECS):
        vec_ref[n] = column(sm_ref[:, D * i : D * (i + 1)].astype(f32))
    part_ref[...] = jnp.zeros_like(part_ref)

    def vec(i):
        return widen(vec_ref[VECS.index(i)], lanes)

    def over_lanes(step):
        def body(c, _):
            step(rows_at(c, lanes))
            return 0

        lax.fori_loop(0, t // lanes, body, 0)

    def norm(r):
        centre = r - jnp.mean(r, axis=0, keepdims=True)
        scale = lax.rsqrt(jnp.mean(centre * centre, axis=0, keepdims=True) + 1e-5)
        return centre * scale, scale

    def norm_back(dy, xh, scale, gain):
        dx = dy * gain
        mean_one = jnp.mean(dx, axis=0, keepdims=True)
        mean_two = jnp.mean(dx * xh, axis=0, keepdims=True)
        return scale * (dx - mean_one - xh * mean_two)

    def first_norm(cs):
        r1 = jnp.transpose(x_ref[cs, :]).astype(f32) + dot(wo_ref[...], o_ref[:, cs], NN) + vec(6)
        xh, scale = norm(r1)
        xh_ref[:, cs] = xh
        rs_ref[:, cs] = scale
        a1 = xh * vec(0) + vec(1)
        a1_ref[:, cs] = a1 + vec(7)
        low_ref[:, cs] = a1.astype(bf)

    over_lanes(first_norm)

    def up_down(j, _):
        rows = rows_at(j, block)
        bias = sm_ref[:, pl.ds(pl.multiple_of(8 * D + j * block, block), block)]
        hid = dot(w1_ref[rows, :], low_ref[...], NN) + widen(column(bias.astype(f32)), t)
        act, slope = gelu_both(hid)
        act = act.astype(bf)
        act_ref[rows, :] = act
        gp_ref[rows, :] = slope.astype(gp_ref.dtype)
        a1_ref[...] += dot(w2_ref[rows, :], act, TN)
        return 0

    lax.fori_loop(0, ff // block, up_down, 0)

    def second_norm(cs):
        xh, scale = norm(a1_ref[:, cs])
        out_ref[cs, :] = jnp.transpose((xh * vec(2) + vec(3)).astype(bf))
        valid = jnp.where(seg_ref[:, cs] >= 0, 1.0, 0.0)
        dy = jnp.transpose(cot_ref[cs, :]).astype(f32) * valid
        dr = norm_back(dy, xh, scale, vec(2))
        a1_ref[:, cs] = dr
        df_ref[:, cs] = dr.astype(bf)
        part_ref[0] += lane_fold(dy * xh)
        part_ref[1] += lane_fold(dy)
        part_ref[2] += lane_fold(dr)

    over_lanes(second_norm)

    def back(j, _):
        rows = rows_at(j, block)
        dh = dot(w2_ref[rows, :], df_ref[...], NN) * gp_ref[rows, :].astype(f32)
        sg_ref[:, pl.ds(pl.multiple_of(8 * D + j * block, block), block)] = fold_row(lane_fold(dh))
        low = dh.astype(bf)
        dw2_ref[rows, :] = dot(act_ref[rows, :], df_ref[...], NT).astype(dw2_ref.dtype)
        dw1_ref[rows, :] = dot(low, low_ref[...], NT).astype(dw1_ref.dtype)
        a1_ref[...] += dot(w1_ref[rows, :], low, TN)
        return 0

    lax.fori_loop(0, ff // block, back, 0)

    def first_back(cs):
        dy = a1_ref[:, cs]
        xh = xh_ref[:, cs]
        dr = norm_back(dy, xh, rs_ref[:, cs], vec(0))
        dr1_ref[:, cs] = dr
        dz = dr.astype(bf)
        low_ref[:, cs] = dz
        part_ref[3] += lane_fold(dy * xh)
        part_ref[4] += lane_fold(dy)
        part_ref[5] += lane_fold(dr)
        do_ref[:, cs] = dot(wo_ref[...], dz, TN).astype(bf)

    over_lanes(first_back)
    dwo_ref[...] = dot(low_ref[...], o_ref[...], NT).astype(dwo_ref.dtype)
    for n, i in enumerate((2, 3, 7, 0, 1, 6)):
        sg_ref[:, D * i : D * (i + 1)] = fold_row(part_ref[n])
    sg_ref[:, 4 * D : 6 * D] = jnp.zeros((1, 2 * D), f32)


def backward_kernel(
    x_ref, seg_ref, w_ref, qkv_ref, o_ref, l_ref, do_ref, dr1_ref,
    dx_ref, dw_ref, db_ref,
    g_ref,
):
    t = x_ref.shape[0]
    q_rows, k_rows = segment_rows(seg_ref[...])

    def head(h, _):
        rows = rows_at(h, HD)
        krow = pl.ds(pl.multiple_of(D + h * HD, HD), HD)
        vrow = pl.ds(pl.multiple_of(2 * D + h * HD, HD), HD)
        q, k, v, do = qkv_ref[rows, :], qkv_ref[krow, :], qkv_ref[vrow, :], do_ref[rows, :]
        inner = jnp.sum(do.astype(f32) * o_ref[rows, :].astype(f32), axis=0, keepdims=True)
        s = dot(
            jnp.concatenate([k, k_rows], 0), jnp.concatenate([q * bf(0.125), q_rows], 0), TN
        )
        p = jnp.exp2((s - l_ref[h]) * LOG2E)
        dp = dot(v, do, TN)
        ds = (p * (dp - inner)).astype(bf)
        g_ref[vrow, :] = dot(do, p.astype(bf), NT).astype(bf)
        g_ref[krow, :] = (dot(q, ds, NT) * 0.125).astype(bf)
        g_ref[rows, :] = (dot(k, ds, NN) * 0.125).astype(bf)
        return 0

    lax.fori_loop(0, HEADS, head, 0)
    block = 256

    def weight_block(i, _):
        rows = rows_at(i, block)
        g = g_ref[rows, :]
        dw_ref[rows, :] = dot(g, x_ref[...], NN).astype(dw_ref.dtype)
        db_ref[:, rows] = fold_row(lane_fold(g.astype(f32)))
        return 0

    lax.fori_loop(0, 3 * D // block, weight_block, 0)

    def input_block(i, _):
        rows = rows_at(i, block)
        dx_ref[rows, :] = jnp.transpose(dr1_ref[:, rows]) + dot(g_ref[:, rows], w_ref[...], TN)
        return 0

    lax.fori_loop(0, t // block, input_block, 0)


def call(kernel, name, outs, scratch, *args):
    return pl.pallas_call(
        kernel,
        out_shape=[jax.ShapeDtypeStruct(s, d) for s, d in outs],
        scratch_shapes=[pltpu.VMEM(s, d) for s, d in scratch],
        compiler_params=pltpu.CompilerParams(vmem_limit_bytes=VMEM_LIMIT),
        name=name,
    )(*args)


def adam_step(weight, grad_sum, first_mom, second_mom, average, decay, rate):
    first_new = 0.9 * first_mom + 0.1 * grad_sum
    second_new = 0.98 * second_mom + 0.02 * grad_sum * grad_sum
    corrected = first_new / (1.0 - 0.9**STEP)
    denominator = jnp.sqrt(second_new / (1.0 - 0.98**STEP)) + 1e-06
    weight_new = weight - rate * (corrected / denominator + decay * weight)
    average_new = 0.75 * average + 0.25 * weight_new
    return (weight_new, first_new, second_new, average_new)


def local(
    features, cotangent, segment_ids, attn_weights, ffn_weights, small_params,
    attn_first, ffn_first, small_first, attn_second, ffn_second, small_second,
    attn_ema, ffn_ema, small_ema,
):
    axes = ("dp", "fsdp")
    t = features.shape[0]
    attn_full = lax.all_gather(attn_weights.astype(bf), axes, axis=0, tiled=True)
    ffn_full = lax.all_gather(ffn_weights.astype(bf), axes, axis=1, tiled=True)
    small_full = lax.all_gather(small_params.astype(bf), axes, axis=0, tiled=True)
    ff = ffn_full.shape[1]
    smalls = small_full.reshape(1, -1)
    seg = segment_ids.reshape(1, t)
    qkv, mixed, logs = call(
        forward_kernel, "attend_forward",
        [((3 * D, t), bf), ((D, t), bf), ((HEADS, 1, t), f32)], [],
        features, seg, attn_full[: 3 * D], smalls,
    )
    outputs, dr1, do, dwo, dw1, dw2, small_grad = call(
        middle_kernel, "middle",
        [((t, D), bf), ((D, t), f32), ((D, t), bf), ((D, D), bf), ((ff, D), bf), ((ff, D), bf),
         ((1, smalls.shape[1]), f32)],
        [((D, t), f32), ((D, t), f32), ((ff, t), bf), ((ff, t), bf), ((1, t), f32), ((D, t), bf),
         ((D, t), bf), ((6, D, 128), f32), ((6, D, 128), f32)],
        features, mixed, cotangent, seg, attn_full[3 * D :], ffn_full[0], ffn_full[1], smalls,
    )
    input_grad, dqkv, bias_grad = call(
        backward_kernel, "attend_backward",
        [((t, D), f32), ((3 * D, D), bf), ((1, 3 * D), f32)], [((3 * D, t), bf)],
        features, seg, attn_full[: 3 * D], qkv, mixed, logs, do, dr1,
    )
    small_grad = small_grad.reshape(-1)
    small_grad = jnp.concatenate(
        [small_grad[: 4 * D], bias_grad[0, :D], bias_grad[0, 2 * D :], small_grad[6 * D :]]
    )
    attn_sum, ffn_sum, small_sum = (
        lax.psum_scatter(jnp.concatenate([dqkv, dwo]), axes, scatter_dimension=0, tiled=True),
        lax.psum_scatter(jnp.stack([dw1, dw2]), axes, scatter_dimension=1, tiled=True),
        lax.psum_scatter(small_grad, axes, scatter_dimension=0, tiled=True),
    )
    attn = adam_step(
        attn_weights, attn_sum.astype(f32), attn_first, attn_second, attn_ema, 0.01, 0.05
    )
    ffn = adam_step(ffn_weights, ffn_sum.astype(f32), ffn_first, ffn_second, ffn_ema, 0.01, 0.05)
    small = adam_step(
        small_params, small_sum, small_first, small_second, small_ema, 0.0, 0.3
    )
    return (outputs, input_grad) + tuple(x for trio in zip(attn, ffn, small) for x in trio)


def solution(mesh):
    row = P(("dp", "fsdp"), None)
    wide = P(None, ("dp", "fsdp"), None)
    flat = P(("dp", "fsdp"))
    state = (row, wide, flat)
    return jax.shard_map(
        local,
        mesh=mesh,
        in_specs=(row, row, flat) + state * 4,
        out_specs=(row, row) + state * 4,
        check_vma=False,
    )
```

time: 829 us -> 547 us (0.66); the launches traced: 820 us -> 547 us
  matrix products: 292 us -> 0 us
  Pallas kernels: 0 us -> 145 us
  other arithmetic: 108 us -> 23.6 us
  local copies, waits for them, and re-layouts: 44.2 us -> 17 us
  waiting for transfers between devices: 273 us -> 264 us
    dot_general x28 -> x0, matrix products: 292 us -> none  [the longest x6 69.4 us: project(): lax.dot_general(left_arg, weight_mat, (((1,), (1,)), ((), ())), preferred...]
    pallas_call x0 -> x3, Pallas kernels: none -> 145 us  [call(): pl.pallas_call(kernel, out_shape=[jax.ShapeDtypeStruct(s, d) for s, d in...]
    reduce_scatter x2, waiting for transfers between devices: 256 us -> 193 us  [the longest x1 139 us: local(): lax.psum_scatter(jnp.stack([dw1, dw2]), axes, scatter_dimension=1, tiled=...]
    all_gather x2, waiting for transfers between devices: 16.8 us -> 71.1 us  [the longest x1 47.9 us: local(): ffn_full = lax.all_gather(ffn_weights.astype(bf), axes, axis=1, tiled=True)]
    convert_element_type x10 -> x3, other arithmetic: 51.2 us -> 4.14 us  [the longest x1 1.81 us: local(): ffn_full = lax.all_gather(ffn_weights.astype(bf), axes, axis=1, tiled=True)]
    reduce_sum x10 -> x0, other arithmetic: 34.7 us -> none  [the longest x2 24.9 us: attend(): row_totals = jnp.sum(expo_vals, axis=-1, keepdims=True)]
    unnamed x135 -> x24, local copies, waits for them, and re-layouts: 20.9 us -> 0.25 us
    while x18 -> x0, local copies, waits for them, and re-layouts: 11.6 us -> none
  transfers between devices with their start and end apart: 4 -> 4, of which waited for: 3 -> 4; matrix products, arithmetic and copies ran while one was open for 17% -> 4% of each run, Pallas kernels for 0% -> 6%
where the time goes in v1:
time: 547 us
  waiting for transfers between devices  264 us (48%)
  Pallas kernels  145 us (27%)
  blocking collectives  82.3 us (15%)
  other arithmetic  23.6 us (4%)
  local copies, waits for them, and re-layouts  17 us (3%)
  between operations  13.9 us (3%)
    pallas_call x3, Pallas kernels, call(): pl.pallas_call(kernel, out_shape=[jax.ShapeDtypeStruct(s, d) for s, d in...  145 us
    reduce_scatter x1, waiting for transfers between devices, local(): lax.psum_scatter(jnp.stack([dw1, dw2]), axes, scatter_dimension=1, tiled=...  139 us
    unnamed x2, blocking collectives  82.3 us
    reduce_scatter x1, waiting for transfers between devices, local(): lax.psum_scatter(jnp.concatenate([dqkv, dwo]), axes, scatter_dimension=0,...  53.6 us
    all_gather x1, waiting for transfers between devices, local(): ffn_full = lax.all_gather(ffn_weights.astype(bf), axes, axis=1, tiled=True)  47.9 us
    all_gather x1, waiting for transfers between devices, local(): lax.all_gather(attn_weights.astype(bf), axes, axis=0, tiled=True)  23.2 us
  transfers between devices with their start and end apart: 4, of which 4 were waited for; matrix products, arithmetic and copies ran while one was open for 4% of the time, Pallas kernels for 6%

profile of v1, /device:TPU:0, one launch (start us, length us, event | category | flops | bytes accessed | tf_op | source)
XLA Modules:
  0.0 546.5 jit_solution(4524329945972752840)
XLA Ops:
  7.2 0.0 all-gather.3.cloned.1.call-start
  7.2 1.6 convert_element_type.15
  8.9 0.0 all-gather.3.cloned.1.call-update
  8.9 0.0 all-gather.5.cloned.1.call-start
  8.9 1.8 convert_element_type.17
  10.8 0.0 all-gather.5.cloned.1.call-update
  10.8 0.0 reduce-scatter.3.cloned.1.call-start
  10.8 0.7 convert_element_type.16
  11.5 0.2 dynamic-update-slice
  11.7 42.3 %all-reduce = bf16[9216]{0:T(1024)(128)(2,1)S(1)} all-reduce(bf16[9216]{0:T(1024)(128)(2,1)S(1)} %dynamic-update-slice), channel_id=1, replica_groups=mesh['dp'=8,'fsdp'=4] {'dp','fsdp'}, use_global_device_ids=true, to_apply=%add | all-reduce | flops 9216 | bytes 36864
  54.0 0.6 reshape.38.sm_ref
  54.6 23.2 %all-gather.3.cloned.1.call-done = bf16[3072,768]{1,0:T(8,128)(2,1)} async-done(((bf16[96,768]{1,0:T(8,128)(2,1)}), bf16[3072,768]{1,0:T(8,128)(2,1)}) %all-gather.3.cloned.1.call-update) | async-done | bytes 4718608 | tf_op jit(solution)/shard_map/all_gather | solution.py:276
  77.9 4.0 slice.41.w_ref
  81.8 30.3 %attend_forward.1 = (bf16[2304,1024]{1,0:T(8,128)(2,1)}, bf16[768,1024]{1,0:T(8,128)(2,1)}, f32[12,1,1024]{2,1,0:T(1,128)}) custom-call(bf16[1024,768]{1,0:T(8,128)(2,1)} %x_ref.5, s32[1,1024]{1,0:T(1,128)} %bitcast.11, bf16[2304,768]{1,0:T(8,128)(2,1)} %slice.41.w_ref, bf16[1,9216]{1,0:T(2,128)(2,1)} %reshape.38.sm_ref), custom_call_target="tpu_custom_call" | custom-call | tf_op jit(solution)/shard_map/attend_forward/pallas_call | solution.py:250
  112.1 2.4 slice.42.wo_ref
  114.5 47.9 %all-gather.5.cloned.1.call-done = bf16[2,3072,768]{2,1,0:T(8,128)(2,1)} async-done(((bf16[2,96,768]{2,1,0:T(8,128)(2,1)}), bf16[2,3072,768]{2,1,0:T(8,128)(2,1)}) %all-gather.5.cloned.1.call-update) | async-done | bytes 9437200 | tf_op jit(solution)/shard_map/all_gather | solution.py:277
  162.4 8.0 %slice_bitcast_fusion = (bf16[3072,768]{1,0:T(8,128)(2,1)}, bf16[3072,768]{1,0:T(8,128)(2,1)}) fusion(bf16[2,3072,768]{2,1,0:T(8,128)(2,1)} %all-gather.5.cloned.1.call-done), kind=kLoop, calls=%fused_computation.1 | loop fusion | bytes 18874368 | tf_op jit(solution)/shard_map/squeeze | solution.py:293
  170.4 62.5 %middle.1 = (bf16[1024,768]{1,0:T(8,128)(2,1)}, f32[768,1024]{1,0:T(8,128)}, bf16[768,1024]{1,0:T(8,128)(2,1)}, bf16[768,768]{1,0:T(8,128)(2,1)}, bf16[3072,768]...) custom-call(bf16[1024,768]{1,0:T(8,128)(2,1)} %x_ref.5, bf16[768,1024]{1,0:T(8,128)(2,1)} %get-tuple-element.27.o_ref, ...), custom_call_target="tpu_custom_call" | custom-call | tf_op jit(solution)/shard_map/middle/pallas_call | solution.py:250
  232.9 52.5 %attend_backward.1 = (f32[1024,768]{1,0:T(8,128)}, bf16[2304,768]{1,0:T(8,128)(2,1)}, f32[1,2304]{1,0:T(1,128)}) custom-call(bf16[1024,768]{1,0:T(8,128)(2,1)} %x_ref.5, s32[1,1024]{1,0:T(1,128)} %bitcast.13, bf16[2304,768]{1,0:T(8,128)(2,1)} %slice.41.w_ref, bf16[2304,1024]{1,0:T(8,128)(2,1)} %get-tuple-element.29.qkv_ref, ...), custom_call_target="tpu_custom_call" | custom-call | tf_op jit(solution)/shard_map/attend_backward/pallas_call | solution.py:250
  285.4 4.4 pad_maximum_fusion.1
  289.9 0.0 reduce-scatter.5.cloned.1.call-start
  290.0 8.2 %pad_maximum_fusion = bf16[2,3072,768]{2,1,0:T(8,128)(2,1)} fusion(bf16[1,3072,768]{2,1,0:T(8,128)(2,1)} %bitcast.9, bf16[1,3072,768]{2,1,0:T(8,128)(2,1)} %bitcast.8), kind=kLoop, calls=%fused_computation | loop fusion | flops 4718592 | bytes 18874368 | tf_op jit(solution)/shard_map/stack | solution.py:306
  298.3 0.0 reduce-scatter.5.cloned.1.call-update
  298.3 0.9 slice.35
  299.2 1.0 slice_reduce_fusion
  300.1 0.6 pad_maximum_fusion.2
  300.8 40.1 %all-reduce.1 = f32[9216]{0:T(1024)} all-reduce(f32[9216]{0:T(1024)} %pad_maximum_fusion.2), channel_id=4, replica_groups=mesh['dp'=8,'fsdp'=4] {'dp','fsdp'}, use_global_device_ids=true, to_apply=%region_2.0.clone | all-reduce | flops 9216 | bytes 73728
  340.8 1.4 multiply_add_fusion.2
  342.2 53.6 %reduce-scatter.3.cloned.1.call-done = bf16[96,768]{1,0:T(8,128)(2,1)} async-done(((bf16[3072,768]{1,0:T(8,128)(2,1)}), bf16[96,768]{1,0:T(8,128)(2,1)}) %reduce-scatter.3.cloned.1.call-update) | async-done | bytes 147472 | tf_op jit(solution)/shard_map/reduce_scatter | solution.py:305
  395.9 2.1 multiply_add_fusion.1
  397.9 139.3 %reduce-scatter.5.cloned.1.call-done = bf16[2,96,768]{2,1,0:T(8,128)(2,1)} async-done(((bf16[2,3072,768]{2,1,0:T(8,128)(2,1)}), bf16[2,96,768]{2,1,0:T(8,128)(2,1)}) %reduce-scatter.5.cloned.1.call-update) | async-done | bytes 294928 | tf_op jit(solution)/shard_map/reduce_scatter | solution.py:306
  537.3 2.7 multiply_add_fusion
  (25 shorter events, 0.1 us)
Async XLA Ops:
  7.2 70.7 %all-gather.3.cloned.1.call-start = ((), (), s32[]{:S(2)}) async-start(), calls=%async_computation.2 | async-start | bytes 4866048 | tf_op jit(solution)/shard_map/all_gather | solution.py:276
  8.9 153.5 %all-gather.5.cloned.1.call-start = ((), (), s32[]{:S(2)}) async-start(), calls=%async_computation.3 | async-start | bytes 9732096 | tf_op jit(solution)/shard_map/all_gather | solution.py:277
  10.8 385.1 %reduce-scatter.3.cloned.1.call-start = ((), (), s32[]{:S(2)}) async-start(), calls=%async_computation.4 | async-start | bytes 4866048 | tf_op jit(solution)/shard_map/reduce_scatter | solution.py:305
  232.9 52.5 %copy-start.1 = (bf16[768,768]{1,0:T(8,128)(2,1)S(1)}, bf16[768,768]{1,0:T(8,128)(2,1)}, u32[]{:S(2)}) copy-start(bf16[768,768]{1,0:T(8,128)(2,1)} %get-tuple-element.35) | copy-start | bytes 3538948
  289.9 247.4 %reduce-scatter.5.cloned.1.call-start = ((), (), s32[]{:S(2)}) async-start(), calls=%async_computation.5 | async-start | bytes 9732096 | tf_op jit(solution)/shard_map/reduce_scatter | solution.py:306
  298.2 1.0 copy-start.10
  298.2 42.7 %copy-start.9 = (f32[288]{0:T(512)S(1)}, f32[288]{0:T(512)}, u32[]{:S(2)}) copy-start(f32[288]{0:T(512)} %param.20) | copy-start | bytes 3460
  298.2 97.7 %copy-start.2 = (f32[96,768]{1,0:T(8,128)S(1)}, f32[96,768]{1,0:T(8,128)}, u32[]{:S(2)}) copy-start(f32[96,768]{1,0:T(8,128)} %param.18) | copy-start | bytes 884740
  298.2 97.7 %copy-start.6 = (f32[96,768]{1,0:T(8,128)S(1)}, f32[96,768]{1,0:T(8,128)}, u32[]{:S(2)}) copy-start(f32[96,768]{1,0:T(8,128)} %param.27) | copy-start | bytes 884740
  298.2 97.7 %copy-start.7 = (f32[96,768]{1,0:T(8,128)S(1)}, f32[96,768]{1,0:T(8,128)}, u32[]{:S(2)}) copy-start(f32[96,768]{1,0:T(8,128)} %param.21) | copy-start | bytes 884740
  298.2 97.6 %copy-start.8 = (f32[96,768]{1,0:T(8,128)S(1)}, f32[96,768]{1,0:T(8,128)}, u32[]{:S(2)}) copy-start(f32[96,768]{1,0:T(8,128)} %param.24) | copy-start | bytes 884740
  298.2 239.1 %copy-start = (f32[2,96,768]{2,1,0:T(8,128)S(1)}, f32[2,96,768]{2,1,0:T(8,128)}, u32[]{:S(2)}) copy-start(f32[2,96,768]{2,1,0:T(8,128)} %param.19) | copy-start | bytes 1769476
  298.2 239.1 %copy-start.3 = (f32[2,96,768]{2,1,0:T(8,128)S(1)}, f32[2,96,768]{2,1,0:T(8,128)}, u32[]{:S(2)}) copy-start(f32[2,96,768]{2,1,0:T(8,128)} %param.28) | copy-start | bytes 1769476
  298.2 239.0 %copy-start.4 = (f32[2,96,768]{2,1,0:T(8,128)S(1)}, f32[2,96,768]{2,1,0:T(8,128)}, u32[]{:S(2)}) copy-start(f32[2,96,768]{2,1,0:T(8,128)} %param.22) | copy-start | bytes 1769476
  298.3 239.0 %copy-start.5 = (f32[2,96,768]{2,1,0:T(8,128)S(1)}, f32[2,96,768]{2,1,0:T(8,128)}, u32[]{:S(2)}) copy-start(f32[2,96,768]{2,1,0:T(8,128)} %param.25) | copy-start | bytes 1769476
Sparse Core Ops, SparseCore 0:
  11.5 66.3 all-gather.2
  81.4 80.9 all-gather.4
  290.0 105.7 reduce-scatter.2
  402.6 134.6 reduce-scatter.4

commit v2 on v1

--- a/solution.py
+++ b/solution.py
@@ -57,7 +57,7 @@
     return ((same - 1.0) * BIG).astype(bf), same.astype(bf)
 
 
-def forward_kernel(x_ref, seg_ref, w_ref, sm_ref, qkv_ref, o_ref, l_ref):
+def plain_forward_kernel(x_ref, seg_ref, w_ref, sm_ref, qkv_ref, o_ref, l_ref):
     t = x_ref.shape[0]
     block = 256
 
@@ -96,10 +96,10 @@
     return h * cdf, cdf + h * pdf
 
 
-VECS = (0, 1, 2, 3, 6, 7)
-
-
-def middle_kernel(
+PLAIN_VECS = (0, 1, 2, 3, 6, 7)
+
+
+def plain_middle_kernel(
     x_ref, o_ref, cot_ref, seg_ref, wo_ref, w1_ref, w2_ref, sm_ref,
     out_ref, dr1_ref, do_ref, dwo_ref, dw1_ref, dw2_ref, sg_ref,
     a1_ref, xh_ref, act_ref, gp_ref, rs_ref, low_ref, df_ref, vec_ref, part_ref,
@@ -107,12 +107,12 @@
     t = x_ref.shape[0]
     ff = w1_ref.shape[0]
     block, lanes = 256, 256
-    for n, i in enumerate(VECS):
+    for n, i in enumerate(PLAIN_VECS):
         vec_ref[n] = column(sm_ref[:, D * i : D * (i + 1)].astype(f32))
     part_ref[...] = jnp.zeros_like(part_ref)
 
     def vec(i):
-        return widen(vec_ref[VECS.index(i)], lanes)
+        return widen(vec_ref[PLAIN_VECS.index(i)], lanes)
 
     def over_lanes(step):
         def body(c, _):
@@ -201,7 +201,7 @@
     sg_ref[:, 4 * D : 6 * D] = jnp.zeros((1, 2 * D), f32)
 
 
-def backward_kernel(
+def plain_backward_kernel(
     x_ref, seg_ref, w_ref, qkv_ref, o_ref, l_ref, do_ref, dr1_ref,
     dx_ref, dw_ref, db_ref,
     g_ref,
@@ -266,11 +266,7 @@
     return (weight_new, first_new, second_new, average_new)
 
 
-def local(
-    features, cotangent, segment_ids, attn_weights, ffn_weights, small_params,
-    attn_first, ffn_first, small_first, attn_second, ffn_second, small_second,
-    attn_ema, ffn_ema, small_ema,
-):
+def gradients_general(features, cotangent, segment_ids, attn_weights, ffn_weights, small_params):
     axes = ("dp", "fsdp")
     t = features.shape[0]
     attn_full = lax.all_gather(attn_weights.astype(bf), axes, axis=0, tiled=True)
@@ -280,12 +276,12 @@
     smalls = small_full.reshape(1, -1)
     seg = segment_ids.reshape(1, t)
     qkv, mixed, logs = call(
-        forward_kernel, "attend_forward",
+        plain_forward_kernel, "attend_forward",
         [((3 * D, t), bf), ((D, t), bf), ((HEADS, 1, t), f32)], [],
         features, seg, attn_full[: 3 * D], smalls,
     )
     outputs, dr1, do, dwo, dw1, dw2, small_grad = call(
-        middle_kernel, "middle",
+        plain_middle_kernel, "plain_middle",
         [((t, D), bf), ((D, t), f32), ((D, t), bf), ((D, D), bf), ((ff, D), bf), ((ff, D), bf),
          ((1, smalls.shape[1]), f32)],
         [((D, t), f32), ((D, t), f32), ((ff, t), bf), ((ff, t), bf), ((1, t), f32), ((D, t), bf),
@@ -293,7 +289,7 @@
         features, mixed, cotangent, seg, attn_full[3 * D :], ffn_full[0], ffn_full[1], smalls,
     )
     input_grad, dqkv, bias_grad = call(
-        backward_kernel, "attend_backward",
+        plain_backward_kernel, "attend_backward",
         [((t, D), f32), ((3 * D, D), bf), ((1, 3 * D), f32)], [((3 * D, t), bf)],
         features, seg, attn_full[: 3 * D], qkv, mixed, logs, do, dr1,
     )
@@ -306,23 +302,727 @@
         lax.psum_scatter(jnp.stack([dw1, dw2]), axes, scatter_dimension=1, tiled=True),
         lax.psum_scatter(small_grad, axes, scatter_dimension=0, tiled=True),
     )
-    attn = adam_step(
-        attn_weights, attn_sum.astype(f32), attn_first, attn_second, attn_ema, 0.01, 0.05
+    return outputs, input_grad, attn_sum.astype(f32), ffn_sum.astype(f32), small_sum
+
+
+MESH = pl.DeviceIdType.MESH
+LAYERS = 4
+
+
+class Place:
+    def __init__(self):
+        zy, xc = lax.axis_index("dp"), lax.axis_index("fsdp")
+        self.z, self.y, self.x, self.c = zy // 2, zy % 2, xc // 2, xc % 2
+        z, y, x, c = self.z, self.y, self.x, self.c
+        self.n1 = (z * 2 + (y + c) % 2, ((x + 1 - c) % 2) * 2 + c)
+        self.n2 = (z * 2 + (y + 1 - c) % 2, ((x + c) % 2) * 2 + c)
+        self.sib = (z * 2 + y, x * 2 + 1 - c)
+        self.n1_yx = ((y + c) % 2, (x + 1 - c) % 2)
+        self.n2_yx = ((y + 1 - c) % 2, (x + c) % 2)
+        self.far_yx = (1 - y, 1 - x)
+        self.is_z = ((3 - z) // 3, (z % 2) * (1 - z // 2), ((z + 1) % 2) * (z // 2), z // 3)
+
+    def pick(self, table):
+        return sum(t * e for t, e in zip(table, self.is_z) if t)
+
+    def at_layer(self, layer):
+        return (layer * 2 + self.y, self.x * 2 + self.c)
+
+
+def greet(peers):
+    barrier = pltpu.get_barrier_semaphore()
+    for peer in peers:
+        pl.semaphore_signal(barrier, inc=1, device_id=peer, device_id_type=MESH)
+    pl.semaphore_wait(barrier, len(peers))
+
+
+class Gather:
+    NEAR = ((0, 1, 2, 3), (1, 0, 1, 2), (2, 2, 3, 1), (3, 3, 0, 0))
+    ONWARD = (None, (0, 2, 3, 0), (0, 0, 1, 0), (0, 0, 3, 0))
+
+    def __init__(self, at, buf, send, recv):
+        self.at, self.buf, self.send, self.recv = at, buf, send, recv
+        self.layer = [at.pick(t) for t in self.NEAR]
+
+    def copy(self, idx, src, dst, peer):
+        ref = self.buf.at[idx]
+        return pltpu.make_async_remote_copy(
+            src_ref=ref, dst_ref=ref, send_sem=self.send.at[src], recv_sem=self.recv.at[dst],
+            device_id=peer, device_id_type=MESH,
+        )
+
+    def mine(self, layer):
+        return (layer, self.at.y, self.at.x, self.at.c)
+
+    def up(self):
+        at = self.at
+        return self.copy(self.mine(at.z), 0, at.z, at.at_layer((at.z + 1) % LAYERS))
+
+    def down(self):
+        at = self.at
+        return self.copy(self.mine(at.z), 1, at.z, at.at_layer((at.z + LAYERS - 1) % LAYERS))
+
+    def onward(self, j):
+        layer = self.layer[j]
+        return self.copy(self.mine(layer), 1 + j, layer, self.at.at_layer(self.at.pick(self.ONWARD[j])))
+
+    def first(self, j):
+        layer = self.layer[j]
+        return self.copy(self.mine(layer), 5 + j, 4 + layer, self.at.n1)
+
+    def second(self, j):
+        layer = self.layer[j]
+        return self.copy(self.mine(layer), 9 + j, 8 + layer, self.at.n2)
+
+    def third(self, j):
+        layer = self.layer[j]
+        return self.copy((layer,) + self.at.n1_yx + (self.at.c,), 13 + j, 12 + layer, self.at.n2)
+
+    def across(self, j):
+        layer = self.layer[j]
+        return self.copy((layer, slice(None), slice(None), self.at.c), 17 + j, 16 + layer, self.at.sib)
+
+    def arrived(self, idx, dst):
+        self.copy(idx, 0, dst, self.at.sib).wait_recv()
+
+    def start_z(self):
+        pl.when(self.at.z < LAYERS - 1)(lambda: self.up().start())
+        pl.when(self.at.z > 0)(lambda: self.down().start())
+
+    def start_xy(self, j=0):
+        self.first(j).start()
+        self.second(j).start()
+
+    def inner(self):
+        return (self.at.z + 1) // 2 == 1
+
+    def z_in(self, j):
+        layer = self.layer[j]
+        self.arrived(self.mine(layer), layer)
+        pl.when(self.inner())(lambda: self.onward(j).start())
+
+    def first_in(self, j):
+        layer = self.layer[j]
+        self.arrived((layer,) + self.at.n1_yx + (self.at.c,), 4 + layer)
+        self.third(j).start()
+
+    def second_in(self, j):
+        layer = self.layer[j]
+        self.arrived((layer,) + self.at.n2_yx + (self.at.c,), 8 + layer)
+        self.arrived((layer,) + self.at.far_yx + (self.at.c,), 12 + layer)
+        self.across(j).start()
+
+    def done(self, j):
+        layer = self.layer[j]
+        self.arrived((layer, slice(None), slice(None), 1 - self.at.c), 16 + layer)
+
+    def drain(self):
+        pl.when(self.at.z < LAYERS - 1)(lambda: self.up().wait_send())
+        pl.when(self.at.z > 0)(lambda: self.down().wait_send())
+        for j in range(LAYERS):
+            if j:
+                pl.when(self.inner())(lambda j=j: self.onward(j).wait_send())
+            for copy in (self.first, self.second, self.third, self.across):
+                copy(j).wait_send()
+
+
+def norm(r):
+    centre = r - jnp.mean(r, axis=0, keepdims=True)
+    scale = lax.rsqrt(jnp.mean(centre * centre, axis=0, keepdims=True) + 1e-5)
+    return centre * scale, scale
+
+
+def forward_kernel(
+    x_ref, seg_ref, aw_ref, fw_ref, smw_ref,
+    aout, fout, sm_ref, qkv_out, o_ref, l_ref, xh_out, rs_ref, low_ref, r2_ref, act_out, gp_out,
+    abuf, fbuf, qkv_ref, xh_ref, act_ref, gp_ref, vec_ref, asend, arecv, fsend, frecv, local_sem,
+):
+    t = x_ref.shape[0]
+    rows = aw_ref.shape[0]
+    n_small = smw_ref.shape[1]
+    at = Place()
+    me = (at.z, at.y, at.x, at.c)
+    abuf[me + (slice(0, rows),)] = aw_ref[...].astype(bf)
+    small = jnp.concatenate([smw_ref[...], jnp.zeros((1, D - n_small), f32)], axis=1)
+    abuf[me + (slice(rows, rows + 16),)] = jnp.broadcast_to(small, (16, D)).astype(bf)
+    attn = Gather(at, abuf, asend, arecv)
+    ffn = Gather(at, fbuf, fsend, frecv)
+    up, down = at.at_layer((at.z + 1) % LAYERS), at.at_layer((at.z + LAYERS - 1) % LAYERS)
+    greet([up, down, at.n1, at.n2, at.sib])
+    attn.start_z()
+    attn.start_xy()
+    fbuf[me + (slice(0, rows),)] = fw_ref[0].astype(bf)
+    fbuf[me + (slice(rows, 2 * rows),)] = fw_ref[1].astype(bf)
+
+    def layer_in(g, j):
+        g.z_in(j)
+        g.start_xy(j)
+
+    layer_in(attn, 1)
+    attn.first_in(0)
+    layer_in(attn, 2)
+    attn.second_in(0)
+    attn.first_in(1)
+    layer_in(attn, 3)
+    attn.done(0)
+    ffn.start_z()
+    attn.second_in(1)
+    attn.first_in(2)
+    attn.done(1)
+    attn.second_in(2)
+    attn.first_in(3)
+    ffn.start_xy()
+    attn.done(2)
+    attn.second_in(3)
+    layer_in(ffn, 1)
+    attn.done(3)
+    for i in range(32):
+        z, y, x, c = i // 8, (i // 4) % 2, (i // 2) % 2, i % 2
+        piece = abuf[z, y, x, c, rows : rows + 16, 0:n_small]
+        sm_ref[:, n_small * i : n_small * (i + 1)] = piece[0:1].astype(f32)
+    aout_copy = pltpu.make_async_copy(abuf, aout, local_sem.at[0])
+    aout_copy.start()
+    for sec in range(3):
+        w = abuf[sec, :, :, :, 0:rows, :].reshape(D, D)
+        p = dot(w, x_ref[...], NT)
+        if sec != 1:
+            o = (4 if sec == 0 else 5) * D
+            p = p + widen(column(sm_ref[:, o : o + D]), t)
+        qkv_ref[sec * D : (sec + 1) * D, :] = p.astype(bf)
+    qkv_copy = pltpu.make_async_copy(qkv_ref, qkv_out, local_sem.at[1])
+    qkv_copy.start()
+    q_rows, k_rows = segment_rows(seg_ref[...])
+    ticks = {
+        2: [lambda: ffn.first_in(0)],
+        3: [lambda: layer_in(ffn, 2)],
+        4: [lambda: ffn.second_in(0)],
+        5: [lambda: ffn.first_in(1), lambda: ffn.done(0)],
+        7: [lambda: layer_in(ffn, 3)],
+        8: [lambda: ffn.second_in(1)],
+        10: [lambda: ffn.first_in(2), lambda: ffn.done(1)],
+    }
+
+    def head(h, _):
+        for k, events in ticks.items():
+
+            @pl.when(h == k)
+            def _(events=events):
+                for event in events:
+                    event()
+
+        r = rows_at(h, HD)
+        q = qkv_ref[r, :] * bf(0.125)
+        k = qkv_ref[pl.ds(pl.multiple_of(D + h * HD, HD), HD), :]
+        v = qkv_ref[pl.ds(pl.multiple_of(2 * D + h * HD, HD), HD), :]
+        s = dot(jnp.concatenate([k, k_rows], 0), jnp.concatenate([q, q_rows], 0), TN)
+        top = jnp.max(s, axis=0, keepdims=True)
+        e = jnp.exp2((s - top) * LOG2E)
+        total = jnp.sum(e, axis=0, keepdims=True)
+        o_ref[r, :] = (dot(v, e.astype(bf), NN) * (1.0 / total)).astype(bf)
+        l_ref[h] = top + jnp.log(total)
+        return 0
+
+    lax.fori_loop(0, HEADS, head, 0)
+    for n, i in enumerate((0, 1, 6, 7)):
+        vec_ref[n] = column(sm_ref[:, D * i : D * (i + 1)])
+    lanes = 256
+
+    def first_norm(i, _):
+        cs = rows_at(i, lanes)
+        wo = abuf[3, :, :, :, 0:rows, :].reshape(D, D)
+        vec = [widen(vec_ref[n], lanes) for n in range(4)]
+        r1 = jnp.transpose(x_ref[cs, :]).astype(f32) + dot(wo, o_ref[:, cs], NN) + vec[2]
+        xh, scale = norm(r1)
+        xh_ref[:, cs] = xh
+        rs_ref[:, cs] = scale
+        a1 = xh * vec[0] + vec[1]
+        r2_ref[:, cs] = a1 + vec[3]
+        low_ref[:, cs] = a1.astype(bf)
+        return 0
+
+    lax.fori_loop(0, t // lanes, first_norm, 0)
+    xh_copy = pltpu.make_async_copy(xh_ref, xh_out, local_sem.at[2])
+    xh_copy.start()
+    half = 4 * rows
+
+    def write_back(j, y):
+        slot = (2 * j + y) % 2
+        where = pl.ds(pl.multiple_of(ffn.layer[j] * 2 * half + y * half, half), half)
+        return [
+            pltpu.make_async_copy(act_ref.at[slot], act_out.at[where], local_sem.at[3 + slot]),
+            pltpu.make_async_copy(gp_ref.at[slot], gp_out.at[where], local_sem.at[5 + slot]),
+        ]
+
+    fout_copies = []
+    for j in range(LAYERS):
+        layer = ffn.layer[j]
+        if j == 0:
+            ffn.second_in(2)
+            ffn.first_in(3)
+        if j == 1:
+            ffn.done(2)
+        if j == 2:
+            ffn.second_in(3)
+        if j == 3:
+            ffn.done(3)
+        fout_copies.append(pltpu.make_async_copy(fbuf.at[layer], fout.at[layer], local_sem.at[7 + j]))
+        fout_copies[-1].start()
+        for y in range(2):
+            slot = (2 * j + y) % 2
+            w1 = fbuf[layer, y, :, :, 0:rows, :].reshape(half, D)
+            w2 = fbuf[layer, y, :, :, rows : 2 * rows, :].reshape(half, D)
+            bias = sm_ref[:, pl.ds(pl.multiple_of(8 * D + layer * 2 * half + y * half, 128), half)]
+            hid = dot(w1, low_ref[...], NN) + widen(column(bias), t)
+            act, slope = gelu_both(hid)
+            act = act.astype(bf)
+            if 2 * j + y >= 2:
+                for copy in write_back((2 * j + y - 2) // 2, y):
+                    copy.wait()
+            act_ref[slot] = act
+            gp_ref[slot] = slope.astype(bf)
+            for copy in write_back(j, y):
+                copy.start()
+            r2_ref[...] += dot(w2, act, TN)
+    for y in range(2):
+        for copy in write_back(LAYERS - 1, y):
+            copy.wait()
+    attn.drain()
+    ffn.drain()
+    for copy in [aout_copy, qkv_copy, xh_copy] + fout_copies:
+        copy.wait()
+
+
+def forward_call(x, seg, aw, fw, smw):
+    t, rows = x.shape[0], aw.shape[0]
+    ff = 32 * rows
+    n = 32 * smw.shape[1]
+    vm, anyw = pl.BlockSpec(memory_space=pltpu.VMEM), pl.BlockSpec(memory_space=pl.ANY)
+    shape = jax.ShapeDtypeStruct
+    sems = pltpu.SemaphoreType.DMA
+    return pl.pallas_call(
+        forward_kernel,
+        name="gather_forward",
+        in_specs=[vm] * 5,
+        out_specs=[anyw, anyw, vm, anyw, vm, vm, anyw, vm, vm, vm, anyw, anyw],
+        out_shape=[
+            shape((4, 2, 2, 2, rows + 16, D), bf), shape((4, 2, 2, 2, 2 * rows, D), bf), shape((1, n), f32),
+            shape((3 * D, t), bf), shape((D, t), bf), shape((HEADS, 1, t), f32), shape((D, t), f32),
+            shape((1, t), f32), shape((D, t), bf), shape((D, t), f32), shape((ff, t), bf), shape((ff, t), bf),
+        ],
+        scratch_shapes=[
+            pltpu.VMEM((4, 2, 2, 2, rows + 16, D), bf), pltpu.VMEM((4, 2, 2, 2, 2 * rows, D), bf),
+            pltpu.VMEM((3 * D, t), bf), pltpu.VMEM((D, t), f32), pltpu.VMEM((2, 4 * rows, t), bf),
+            pltpu.VMEM((2, 4 * rows, t), bf), pltpu.VMEM((4, D, 128), f32),
+            sems((21,)), sems((20,)), sems((21,)), sems((20,)), sems((11,)),
+        ],
+        compiler_params=pltpu.CompilerParams(
+            vmem_limit_bytes=VMEM_LIMIT, collective_id=0, has_side_effects=True
+        ),
+    )(x, seg, aw, fw, smw)
+
+
+def norm_back(dy, xh, scale, gain):
+    dx = dy * gain
+    mean_one = jnp.mean(dx, axis=0, keepdims=True)
+    mean_two = jnp.mean(dx * xh, axis=0, keepdims=True)
+    return scale * (dx - mean_one - xh * mean_two)
+
+
+VECS = (0, 2, 3)
+
+
+def middle_kernel(
+    cot_ref, seg_ref, o_ref, xh_ref, rs_ref, low_ref, r2_ref, sm_ref, wo_ref, w_ref, act_ref, gp_ref,
+    out_ref, dr1_ref, do_ref, dwo_ref, dw_ref, sg_ref,
+    acc_ref, df_ref, vec_ref, part_ref,
+):
+    step = pl.program_id(0)
+    t = cot_ref.shape[0]
+    rows = w_ref.shape[4] // 2
+    half = 4 * rows
+    lanes = 256
+
+    def vec(i):
+        return widen(vec_ref[VECS.index(i)], lanes)
+
+    def over_lanes(piece):
+        def body(c, _):
+            piece(rows_at(c, lanes))
+            return 0
+
+        lax.fori_loop(0, t // lanes, body, 0)
+
+    @pl.when(step == 0)
+    def _():
+        for n, i in enumerate(VECS):
+            vec_ref[n] = column(sm_ref[:, D * i : D * (i + 1)])
+        part_ref[...] = jnp.zeros_like(part_ref)
+
+        def second_norm(cs):
+            xh, scale = norm(r2_ref[:, cs])
+            out_ref[cs, :] = jnp.transpose((xh * vec(2) + vec(3)).astype(bf))
+            valid = jnp.where(seg_ref[:, cs] >= 0, 1.0, 0.0)
+            dy = jnp.transpose(cot_ref[cs, :]).astype(f32) * valid
+            dr = norm_back(dy, xh, scale, vec(2))
+            acc_ref[:, cs] = dr
+            df_ref[:, cs] = dr.astype(bf)
+            part_ref[0] += lane_fold(dy * xh)
+            part_ref[1] += lane_fold(dy)
+            part_ref[2] += lane_fold(dr)
+
+        over_lanes(second_norm)
+
+    w1 = w_ref[0, 0, :, :, 0:rows, :].reshape(half, D)
+    w2 = w_ref[0, 0, :, :, rows : 2 * rows, :].reshape(half, D)
+    dh = dot(w2, df_ref[...], NN) * gp_ref[...].astype(f32)
+    sg_ref[:, pl.ds(pl.multiple_of(8 * D + step * half, 128), half)] = fold_row(lane_fold(dh))
+    low = dh.astype(bf)
+    dw2 = dot(act_ref[...], df_ref[...], NT).astype(bf)
+    dw1 = dot(low, low_ref[...], NT).astype(bf)
+    for x in range(2):
+        for c in range(2):
+            at = slice((2 * x + c) * rows, (2 * x + c + 1) * rows)
+            dw_ref[0, 0, x, c, 0:rows, :] = dw1[at]
+            dw_ref[0, 0, x, c, rows : 2 * rows, :] = dw2[at]
+    acc_ref[...] += dot(w1, low, TN)
+
+    @pl.when(step == pl.num_programs(0) - 1)
+    def _():
+        wo = wo_ref[0, :, :, :, 0:rows, :].reshape(D, D)
+
+        def first_back(cs):
+            dy = acc_ref[:, cs]
+            xh = xh_ref[:, cs]
+            dr = norm_back(dy, xh, rs_ref[:, cs], vec(0))
+            dr1_ref[:, cs] = dr
+            dz = dr.astype(bf)
+            df_ref[:, cs] = dz
+            part_ref[3] += lane_fold(dy * xh)
+            part_ref[4] += lane_fold(dy)
+            part_ref[5] += lane_fold(dr)
+            do_ref[:, cs] = dot(wo, dz, TN).astype(bf)
+
+        over_lanes(first_back)
+        dwo_ref[...] = dot(df_ref[...], o_ref[...], NT).astype(bf)
+        for n, i in enumerate((2, 3, 7, 0, 1, 6)):
+            sg_ref[:, D * i : D * (i + 1)] = fold_row(part_ref[n])
+        sg_ref[:, 4 * D : 6 * D] = jnp.zeros((1, 2 * D), f32)
+
+
+def middle_call(cot, seg, o, xh, rs, low, r2, sm, abuf, fbuf, act, gp):
+    t = cot.shape[0]
+    rows = fbuf.shape[4] // 2
+    half = 4 * rows
+    shape = jax.ShapeDtypeStruct
+
+    def whole(a):
+        return pl.BlockSpec(a.shape, lambda j: (0,) * len(a.shape))
+
+    wspec = pl.BlockSpec((1, 1, 2, 2, 2 * rows, D), lambda j: (j // 2, j % 2, 0, 0, 0, 0))
+    rspec = pl.BlockSpec((half, t), lambda j: (j, 0))
+    outs = [
+        shape((t, D), bf), shape((D, t), f32), shape((D, t), bf), shape((D, D), bf), shape(fbuf.shape, bf),
+        shape(sm.shape, f32),
+    ]
+    return pl.pallas_call(
+        middle_kernel,
+        name="middle",
+        grid=(8,),
+        in_specs=[whole(a) for a in (cot, seg, o, xh, rs, low, r2, sm)]
+        + [pl.BlockSpec((1,) + abuf.shape[1:], lambda j: (3, 0, 0, 0, 0, 0)), wspec, rspec, rspec],
+        out_specs=[whole(a) for a in outs[:4]] + [wspec, whole(outs[5])],
+        out_shape=outs,
+        scratch_shapes=[
+            pltpu.VMEM((D, t), f32), pltpu.VMEM((D, t), bf), pltpu.VMEM((3, D, 128), f32),
+            pltpu.VMEM((6, D, 128), f32),
+        ],
+        compiler_params=pltpu.CompilerParams(vmem_limit_bytes=VMEM_LIMIT),
+    )(cot, seg, o, xh, rs, low, r2, sm, abuf, fbuf, act, gp)
+
+
+class Scatter:
+    def __init__(self, at, own, cross, pair, single, along, send, recv):
+        self.at, self.own, self.cross, self.pair, self.single, self.along = at, own, cross, pair, single, along
+        self.send, self.recv = send, recv
+        self.p = (1 - at.c) * at.x + at.c * at.y
+
+    def copy(self, src, dst, kind, layer, peer, land=None):
+        land = layer if land is None else land
+        return pltpu.make_async_remote_copy(
+            src_ref=src, dst_ref=dst, send_sem=self.send.at[kind * LAYERS + layer],
+            recv_sem=self.recv.at[kind * LAYERS + land], device_id=peer, device_id_type=MESH,
+        )
+
+    def across(self, layer, src):
+        return self.copy(src, self.cross.at[layer], 0, layer, self.at.sib)
+
+    def far(self, layer):
+        return self.copy(
+            self.own.at[(layer,) + self.at.far_yx], self.pair.at[layer, 1 - self.p], 1, layer, self.at.n2
+        )
+
+    def near(self, layer):
+        return self.copy(self.own.at[(layer,) + self.at.n2_yx], self.pair.at[layer, self.p], 2, layer, self.at.n2)
+
+    def first(self, layer):
+        return self.copy(self.own.at[(layer,) + self.at.n1_yx], self.single.at[layer], 3, layer, self.at.n1)
+
+    def to_layer(self, layer):
+        return self.copy(
+            self.own.at[layer, self.at.y, self.at.x], self.along.at[self.at.z], 4, layer,
+            self.at.at_layer(layer), self.at.z,
+        )
+
+    def add(self, where, ref):
+        self.own[where] = (self.own[where].astype(f32) + ref[...].astype(f32)).astype(bf)
+
+    def cross_in(self, layer):
+        self.across(layer, self.cross.at[layer]).wait_recv()
+        for yx in (self.at.far_yx, self.at.n2_yx, self.at.n1_yx, (self.at.y, self.at.x)):
+            self.add((layer,) + yx, self.cross.at[(layer,) + yx])
+            if yx is self.at.far_yx:
+                self.far(layer).start()
+            if yx is self.at.n2_yx:
+                self.near(layer).start()
+
+    def pair_in(self, layer):
+        self.far(layer).wait_recv()
+        self.add((layer,) + self.at.n1_yx, self.pair.at[layer, 1 - self.p])
+        self.first(layer).start()
+        self.near(layer).wait_recv()
+        self.add((layer, self.at.y, self.at.x), self.pair.at[layer, self.p])
+
+    def single_in(self, layer):
+        self.first(layer).wait_recv()
+        self.add((layer, self.at.y, self.at.x), self.single.at[layer])
+        pl.when(layer != self.at.z)(lambda: self.to_layer(layer).start())
+
+    def finish(self):
+        at = self.at
+        total = self.own[at.z, at.y, at.x].astype(f32)
+        for d in (1, 2, 3):
+            layer = (at.z + d) % LAYERS
+            self.copy(self.along.at[layer], self.along.at[layer], 4, layer, at.sib).wait_recv()
+            total = total + self.along[layer].astype(f32)
+        return total
+
+    def drain(self, layer, src):
+        self.across(layer, src).wait_send()
+        self.far(layer).wait_send()
+        self.near(layer).wait_send()
+        self.first(layer).wait_send()
+        pl.when(layer != self.at.z)(lambda: self.to_layer(layer).wait_send())
+
+
+CQ = 512
+
+
+def backward_kernel(
+    x_ref, seg_ref, qkv_ref, o_ref, l_ref, do_ref, dwo_ref, sg_ref, dwf, abuf, dr1,
+    dx, gf_ref, ga_ref,
+    g_ref, dwa, w_ref, dr1_ref, dx_ref, small_ref,
+    fown, fcross, fpair, fsingle, falong, across_ref, apair, asingle, aalong, aown,
+    fsend, frecv, asend, arecv, local_sem,
+):
+    t = x_ref.shape[0]
+    at = Place()
+    rows = w_ref.shape[4]
+    n_small = small_ref.shape[1] // 32
+    z_layers = [(at.z + d) % LAYERS for d in range(LAYERS)]
+    order = [z_layers[d] for d in (2, 1, 3, 0)]
+    ffn = Scatter(at, fown, fcross, fpair, fsingle, falong, fsend, frecv)
+    attn = Scatter(at, aown, across_ref, apair, asingle, aalong, asend, arecv)
+
+    def ffn_src(layer):
+        return dwf.at[layer, :, :, 1 - at.c]
+
+    def attn_src(layer):
+        return dwa.at[layer, :, :, 1 - at.c]
+
+    loads = []
+    for n, layer in enumerate(order):
+        loads.append(pltpu.make_async_copy(dwf.at[layer, :, :, at.c], fown.at[layer], local_sem.at[n]))
+        loads[-1].start()
+    w_copy = pltpu.make_async_copy(abuf.at[0:3, :, :, :, 0:rows, :], w_ref, local_sem.at[4])
+    w_copy.start()
+    dr1_copy = pltpu.make_async_copy(dr1, dr1_ref, local_sem.at[5])
+    dr1_copy.start()
+    greet([at.at_layer(layer) for layer in z_layers[1:]] + [at.n1, at.n2, at.sib])
+    for layer in order:
+        ffn.across(layer, ffn_src(layer)).start()
+
+    def small_rows(layer, y, x, c):
+        i = layer * 8 + y * 4 + x * 2 + c
+        piece = jnp.concatenate(
+            [small_ref[:, i * n_small : (i + 1) * n_small], jnp.zeros((1, D - n_small), f32)], axis=1
+        )
+        return jnp.broadcast_to(piece, (16, D)).astype(bf)
+
+    def fill(layer, dw):
+        for y in range(2):
+            for x in range(2):
+                for c in range(2):
+                    i = y * 4 + x * 2 + c
+                    dwa[layer, y, x, c, 0:rows, :] = dw[i * rows : (i + 1) * rows]
+                    dwa[layer, y, x, c, rows : rows + 16, :] = small_rows(layer, y, x, c)
+        aown[layer] = dwa[layer, :, :, pl.ds(at.c, 1)].reshape(2, 2, rows + 16, D)
+        attn.across(layer, attn_src(layer)).start()
+
+    small_ref[...] = sg_ref[...]
+    fill(3, dwo_ref[...])
+    q_rows, k_rows = segment_rows(seg_ref[...])
+
+    def ffn_cross(n):
+        loads[n].wait()
+        ffn.cross_in(order[n])
+
+    ticks = {
+        1: [lambda: ffn_cross(0)],
+        2: [lambda: ffn_cross(1)],
+        3: [lambda: ffn.pair_in(order[0]), lambda: ffn_cross(2)],
+        4: [lambda: ffn_cross(3)],
+        5: [lambda: ffn.single_in(order[0]), lambda: ffn.pair_in(order[1])],
+        7: [lambda: ffn.single_in(order[1]), lambda: ffn.pair_in(order[2])],
+        9: [lambda: ffn.single_in(order[2]), lambda: ffn.pair_in(order[3])],
+        10: [lambda: attn.cross_in(3)],
+        11: [lambda: ffn.single_in(order[3])],
+    }
+
+    def head(h, _):
+        for k, events in ticks.items():
+
+            @pl.when(h == k)
+            def _(events=events):
+                for event in events:
+                    event()
+
+        hrows = rows_at(h, HD)
+        krow = pl.ds(pl.multiple_of(D + h * HD, HD), HD)
+        vrow = pl.ds(pl.multiple_of(2 * D + h * HD, HD), HD)
+        q, k, v, do = qkv_ref[hrows, :], qkv_ref[krow, :], qkv_ref[vrow, :], do_ref[hrows, :]
+        inner = jnp.sum(do.astype(f32) * o_ref[hrows, :].astype(f32), axis=0, keepdims=True)
+        lrow = l_ref[h]
+        keys = jnp.concatenate([k, k_rows], 0)
+        queries = jnp.concatenate([q * bf(0.125), q_rows], 0)
+        dv = dk = 0.0
+        for i in range(t // CQ):
+            cs = slice(i * CQ, (i + 1) * CQ)
+            s = dot(keys, queries[:, cs], TN)
+            p = jnp.exp2((s - lrow[:, cs]) * LOG2E)
+            dp = dot(v, do[:, cs], TN)
+            ds = (p * (dp - inner[:, cs])).astype(bf)
+            dv = dv + dot(do[:, cs], p.astype(bf), NT)
+            dk = dk + dot(q[:, cs], ds, NT)
+            g_ref[hrows, cs] = (dot(k, ds, NN) * 0.125).astype(bf)
+        g_ref[vrow, :] = dv.astype(bf)
+        g_ref[krow, :] = (dk * 0.125).astype(bf)
+        return 0
+
+    lax.fori_loop(0, HEADS, head, 0)
+    for sec in (0, 2):
+        part = lane_fold(g_ref[sec * D : (sec + 1) * D, :].astype(f32))
+        o = (4 if sec == 0 else 5) * D
+        small_ref[:, o : o + D] = fold_row(part)
+    for layer in range(3):
+        fill(layer, dot(g_ref[layer * D : (layer + 1) * D, :], x_ref[...], NN).astype(bf))
+    attn.pair_in(3)
+    for layer in range(3):
+        attn.cross_in(layer)
+    attn.single_in(3)
+    w_copy.wait()
+    dr1_copy.wait()
+    lanes = 256
+
+    def input_block(i, _):
+        cs = rows_at(i, lanes)
+        w = w_ref[...].reshape(3 * D, D)
+        dx_ref[cs, :] = jnp.transpose(dr1_ref[:, cs]) + dot(g_ref[:, cs], w, TN)
+        return 0
+
+    lax.fori_loop(0, t // lanes, input_block, 0)
+    dx_copy = pltpu.make_async_copy(dx_ref, dx, local_sem.at[6])
+    dx_copy.start()
+    gf_ref[...] = ffn.finish()
+    for layer in range(3):
+        attn.pair_in(layer)
+    for layer in range(3):
+        attn.single_in(layer)
+    ga_ref[...] = attn.finish()
+    for layer in range(LAYERS):
+        ffn.drain(layer, ffn_src(layer))
+        attn.drain(layer, attn_src(layer))
+    dx_copy.wait()
+
+
+def backward_call(x, seg, qkv, o, logs, do, dwo, sg, dwf, abuf, dr1):
+    t = x.shape[0]
+    ra, rf = abuf.shape[4], dwf.shape[4]
+    vm, anyw = pl.BlockSpec(memory_space=pltpu.VMEM), pl.BlockSpec(memory_space=pl.ANY)
+    shape = jax.ShapeDtypeStruct
+    sems = pltpu.SemaphoreType.DMA
+
+    def buffers(r):
+        return [
+            pltpu.VMEM((4, 2, 2, r, D), bf), pltpu.VMEM((4, 2, r, D), bf), pltpu.VMEM((4, r, D), bf),
+            pltpu.VMEM((4, r, D), bf),
+        ]
+
+    return pl.pallas_call(
+        backward_kernel,
+        name="backward_scatter",
+        in_specs=[vm] * 8 + [anyw] * 3,
+        out_specs=[anyw, vm, vm],
+        out_shape=[shape((t, D), f32), shape((rf, D), f32), shape((ra, D), f32)],
+        scratch_shapes=[
+            pltpu.VMEM((3 * D, t), bf), pltpu.VMEM(abuf.shape, bf), pltpu.VMEM((3, 2, 2, 2, ra - 16, D), bf),
+            pltpu.VMEM((D, t), f32), pltpu.VMEM((t, D), f32), pltpu.VMEM(sg.shape, f32),
+            pltpu.VMEM((4, 2, 2, rf, D), bf),
+        ]
+        + buffers(rf)
+        + buffers(ra)
+        + [pltpu.VMEM((4, 2, 2, ra, D), bf), sems((20,)), sems((20,)), sems((20,)), sems((20,)), sems((7,))],
+        compiler_params=pltpu.CompilerParams(
+            vmem_limit_bytes=VMEM_LIMIT, collective_id=1, has_side_effects=True
+        ),
+    )(x, seg, qkv, o, logs, do, dwo, sg, dwf, abuf, dr1)
+
+
+def gradients_block(features, cotangent, segment_ids, attn_weights, ffn_weights, small_params):
+    t, rows = features.shape[0], attn_weights.shape[0]
+    seg = segment_ids.reshape(1, t)
+    abuf, fbuf, sm, qkv, o, logs, xh, rs, low, r2, act, gp = forward_call(
+        features, seg, attn_weights, ffn_weights, small_params.reshape(1, -1)
     )
-    ffn = adam_step(ffn_weights, ffn_sum.astype(f32), ffn_first, ffn_second, ffn_ema, 0.01, 0.05)
-    small = adam_step(
-        small_params, small_sum, small_first, small_second, small_ema, 0.0, 0.3
+    outputs, dr1, do, dwo, dwf, sg = middle_call(cotangent, seg, o, xh, rs, low, r2, sm, abuf, fbuf, act, gp)
+    input_grad, gf, ga = backward_call(features, seg, qkv, o, logs, do, dwo, sg, dwf, abuf, dr1)
+    small_sum = ga[rows, : small_params.shape[0]]
+    return outputs, input_grad, ga[:rows], gf.reshape(2, rows, D), small_sum
+
+
+def local(
+    gradients,
+    features, cotangent, segment_ids, attn_weights, ffn_weights, small_params,
+    attn_first, ffn_first, small_first, attn_second, ffn_second, small_second,
+    attn_ema, ffn_ema, small_ema,
+):
+    outputs, input_grad, attn_sum, ffn_sum, small_sum = gradients(
+        features, cotangent, segment_ids, attn_weights, ffn_weights, small_params
     )
+    attn = adam_step(attn_weights, attn_sum, attn_first, attn_second, attn_ema, 0.01, 0.05)
+    ffn = adam_step(ffn_weights, ffn_sum, ffn_first, ffn_second, ffn_ema, 0.01, 0.05)
+    small = adam_step(small_params, small_sum, small_first, small_second, small_ema, 0.0, 0.3)
     return (outputs, input_grad) + tuple(x for trio in zip(attn, ffn, small) for x in trio)
 
 
 def solution(mesh):
+    block = mesh.shape["dp"] == 8 and mesh.shape["fsdp"] == 4
+    gradients = gradients_block if block else gradients_general
     row = P(("dp", "fsdp"), None)
     wide = P(None, ("dp", "fsdp"), None)
     flat = P(("dp", "fsdp"))
     state = (row, wide, flat)
     return jax.shard_map(
-        local,
+        partial(local, gradients),
         mesh=mesh,
         in_specs=(row, row, flat) + state * 4,
         out_specs=(row, row) + state * 4,

time: 547 us -> 258 us (0.47)
  waiting for transfers between devices: 264 us -> 0 us
  Pallas kernels: 145 us -> 242 us
  blocking collectives: 82.3 us -> 0 us
  other arithmetic: 23.6 us -> 5.68 us
  local copies, waits for them, and re-layouts: 17 us -> 3.71 us
  between operations: 13.9 us -> 1.26 us
    reduce_scatter x2 -> x0, waiting for transfers between devices: 193 us -> none  [the longest x1 139 us: local(): lax.psum_scatter(jnp.stack([dw1, dw2]), axes, scatter_dimension=1, tiled=...]
    pallas_call x3, Pallas kernels: 145 us -> 242 us  [the longest x1 104 us: forward_call(): pl.pallas_call(forward_kernel, name='gather_forward', in_specs=[vm] * 5,...]
    unnamed x2 -> x0, blocking collectives: 82.3 us -> none
    all_gather x2 -> x0, waiting for transfers between devices: 71.1 us -> none  [the longest x1 47.9 us: local(): ffn_full = lax.all_gather(ffn_weights.astype(bf), axes, axis=1, tiled=True)]
    another operation x1 -> x0, other arithmetic: 8.22 us -> none  [local(): jnp.stack([dw1, dw2])]
    squeeze x1 -> x0, local copies, waits for them, and re-layouts: 7.95 us -> none  [local(): ffn_full[1]]
    slice x5 -> x1, local copies, waits for them, and re-layouts: 8.18 us -> 0.73 us  [gradients_block(): small_sum = ga[rows, :small_params.shape[0]]]
  transfers between devices with their start and end apart: 4 -> 0, of which waited for: 4 -> 0; matrix products, arithmetic and copies ran while one was open for 4% -> 0% of each run, Pallas kernels for 6% -> 0%
where the time goes in v2:
time: 258 us; the launch traced here: 253 us
  Pallas kernels  242 us (94%)
  other arithmetic  5.68 us (2%)
  local copies, waits for them, and re-layouts  3.71 us (1%)
    pallas_call x1, Pallas kernels, forward_call(): pl.pallas_call(forward_kernel, name='gather_forward', in_specs=[vm] * 5,...  104 us
    pallas_call x1, Pallas kernels, backward_call(): pl.pallas_call(backward_kernel, name='backward_scatter', in_specs=[vm] *...  94.4 us
    pallas_call x1, Pallas kernels, middle_call(): pl.pallas_call(middle_kernel, name='middle', grid=(8,), in_specs=[whole(a...  43.6 us
    add x3, other arithmetic, adam_step(): average_new = 0.75 * average + 0.25 * weight_new  5.68 us

profile of v2, /device:TPU:0, one launch (start us, length us, event | category | flops | bytes accessed | tf_op | source)
XLA Modules:
  0.0 253.0 jit_solution(3029692864308632765)
XLA Ops:
  0.6 1.2 reshape.38.smw_ref
  1.9 104.4 %gather_forward.1 = (bf16[4,2,2,2,112,768]{5,4,3,2,1,0:T(8,128)(2,1)}, bf16[4,2,2,2,192,768]{5,4,3,2,1,0:T(8,128)(2,1)}, f32[1,9216]{1,0:T(1,128)}, bf16[2304,10...) custom-call(bf16[1024,768]{1,0:T(8,128)(2,1)} %x_ref.3, ...), custom_call_target="tpu_custom_call" | custom-call | tf_op jit(solution)/shard_map/gather_forward/pallas_call | solution.py:602
  106.3 43.6 %middle.1 = (bf16[1024,768]{1,0:T(8,128)(2,1)}, f32[768,1024]{1,0:T(8,128)}, bf16[768,1024]{1,0:T(8,128)(2,1)}, bf16[768,768]{1,0:T(8,128)(2,1)}, bf16[4,2,2,2,1...) custom-call(bf16[1024,768]{1,0:T(8,128)(2,1)} %cot_ref.1, s32[1,1024]{1,0:T(1,128)} %bitcast.4, ...), custom_call_target="tpu_custom_call" | custom-call | tf_op jit(solution)/shard_map/middle/pallas_call | solution.py:727
  149.9 0.0 copy-start.10
  149.9 0.0 copy-start.11
  149.9 0.0 copy-start.12
  149.9 0.0 copy-start.2
  149.9 0.0 copy-start.6
  149.9 0.0 copy-start.7
  150.0 0.0 copy-start.8
  150.0 0.0 copy-start.1
  150.0 0.0 copy-start.3
  150.0 0.0 copy-start.4
  150.0 0.0 copy-start.5
  150.0 94.4 %backward_scatter.1 = (f32[1024,768]{1,0:T(8,128)}, f32[192,768]{1,0:T(8,128)}, f32[112,768]{1,0:T(8,128)}) custom-call(bf16[1024,768]{1,0:T(8,128)(2,1)} %x_ref.3, s32[1,1024]{1,0:T(1,128)} %bitcast.5, bf16[2304,1024]{1,0:T(8,128)(2,1)} %get-tuple-element.46.qkv_ref, bf16[768,1024]{1,0:T(8,128)(2,1)} %get-tuple-element.35.o_ref, ...), custom_call_target="tpu_custom_call" | custom-call | tf_op jit(solution)/shard_map/backward_scatter/pallas_call | solution.py:970
  244.4 0.7 slice_reduce_fusion
  245.1 0.0 copy-done.9
  245.2 0.0 copy-done.10
  245.2 0.0 copy-done.11
  245.2 0.0 copy-done.12
  245.2 0.6 multiply_add_fusion.4
  245.8 0.0 copy-done.2
  245.8 0.0 copy-done.6
  245.8 0.0 copy-done.7
  245.8 0.0 copy-done.8
  245.8 2.1 multiply_add_fusion.2
  247.9 0.0 copy-done.1
  247.9 0.0 copy-done.3
  248.0 0.0 copy-done.4
  248.0 0.0 copy-done.5
  248.0 2.9 %multiply_add_fusion = (f32[2,96,768]{2,1,0:T(8,128)}, f32[2,96,768]{2,1,0:T(8,128)}, f32[2,96,768]{2,1,0:T(8,128)}, f32[2,96,768]{2,1,0:T(8,128)}) fusion(f32[2,96,768]{2,1,0:T(8,128)S(1)} %copy-done.3, f32[2,96,768]{2,1,0:T(8,128)S(1)} %copy-done.1, f32[2,96,768]{2,1,0:T(8,128)} %bitcast.2, f32[2,96,768]{2,1,0:T(8,128)S(1)} %copy-done.4, ...), kind=kLoop, calls=%fused_computation.2 | loop fusion | flops 2654208 | bytes 5308416 | tf_op jit(solution)/shard_map/add | solution.py:265
  250.9 1.7 copy.30
  (3 shorter events, 0.0 us)
Async XLA Ops:
  149.9 95.3 %copy-start.9 = (f32[288]{0:T(512)S(1)}, f32[288]{0:T(512)}, u32[]{:S(2)}) copy-start(f32[288]{0:T(512)} %param.20) | copy-start | bytes 3460
  149.9 95.3 %copy-start.10 = (f32[288]{0:T(512)S(1)}, f32[288]{0:T(512)}, u32[]{:S(2)}) copy-start(f32[288]{0:T(512)} %param.29) | copy-start | bytes 3460
  149.9 95.3 %copy-start.11 = (f32[288]{0:T(512)S(1)}, f32[288]{0:T(512)}, u32[]{:S(2)}) copy-start(f32[288]{0:T(512)} %param.23) | copy-start | bytes 3460
  149.9 95.3 %copy-start.12 = (f32[288]{0:T(512)S(1)}, f32[288]{0:T(512)}, u32[]{:S(2)}) copy-start(f32[288]{0:T(512)} %param.26) | copy-start | bytes 3460
  149.9 95.9 %copy-start.2 = (f32[96,768]{1,0:T(8,128)S(1)}, f32[96,768]{1,0:T(8,128)}, u32[]{:S(2)}) copy-start(f32[96,768]{1,0:T(8,128)} %aw_ref.1) | copy-start | bytes 884740
  149.9 95.9 %copy-start.6 = (f32[96,768]{1,0:T(8,128)S(1)}, f32[96,768]{1,0:T(8,128)}, u32[]{:S(2)}) copy-start(f32[96,768]{1,0:T(8,128)} %param.27) | copy-start | bytes 884740
  149.9 95.9 %copy-start.7 = (f32[96,768]{1,0:T(8,128)S(1)}, f32[96,768]{1,0:T(8,128)}, u32[]{:S(2)}) copy-start(f32[96,768]{1,0:T(8,128)} %param.21) | copy-start | bytes 884740
  150.0 95.8 %copy-start.8 = (f32[96,768]{1,0:T(8,128)S(1)}, f32[96,768]{1,0:T(8,128)}, u32[]{:S(2)}) copy-start(f32[96,768]{1,0:T(8,128)} %param.24) | copy-start | bytes 884740
  150.0 98.0 %copy-start.1 = (f32[2,96,768]{2,1,0:T(8,128)S(1)}, f32[2,96,768]{2,1,0:T(8,128)}, u32[]{:S(2)}) copy-start(f32[2,96,768]{2,1,0:T(8,128)} %fw_ref.1) | copy-start | bytes 1769476
  150.0 98.0 %copy-start.3 = (f32[2,96,768]{2,1,0:T(8,128)S(1)}, f32[2,96,768]{2,1,0:T(8,128)}, u32[]{:S(2)}) copy-start(f32[2,96,768]{2,1,0:T(8,128)} %param.28) | copy-start | bytes 1769476
  150.0 98.0 %copy-start.4 = (f32[2,96,768]{2,1,0:T(8,128)S(1)}, f32[2,96,768]{2,1,0:T(8,128)}, u32[]{:S(2)}) copy-start(f32[2,96,768]{2,1,0:T(8,128)} %param.22) | copy-start | bytes 1769476
  150.0 98.0 %copy-start.5 = (f32[2,96,768]{2,1,0:T(8,128)S(1)}, f32[2,96,768]{2,1,0:T(8,128)}, u32[]{:S(2)}) copy-start(f32[2,96,768]{2,1,0:T(8,128)} %param.25) | copy-start | bytes 1769476
  247.9 3.0 %copy-start = (f32[1024,768]{1,0:T(8,128)S(1)}, f32[1024,768]{1,0:T(8,128)}, u32[]{:S(2)}) copy-start(f32[1024,768]{1,0:T(8,128)} %get-tuple-element.83) | copy-start | bytes 9437188
